TPU v7x, 256 devices: a whole 4x4x8 slice. The times are simulated.
256 devices in a mesh: expert: 64 (over z, y, core), mp: 4 (over x).
Axes of the slice: x: 4, y: 4, z: 8, core: 2. Of those that a mesh axis runs over, the one named last changes fastest.
Arguments:
- attn: bfloat16 [8192, 2048], P('expert', 'mp'), may hold values from -16 to 16
- out_proj: bfloat16 [2048, 2048], P('mp'), may hold values from -0.125 to 0.125
- tangent_proj: bfloat16 [2048, 2048], P('mp'), may hold values from -0.125 to 0.125
- resid: bfloat16 [8192, 2048], P('expert', 'mp'), may hold values from -6 to 6
- target: bfloat16 [8192, 2048], P('expert', 'mp'), may hold values from -6 to 6
- routes: int32 [8192, 2], P('expert'), may hold values from 0 to 63, all different within a row; in each aligned block of 128 rows (0 to 127, 128 to 255, ...) at most 5 rows name the same one
- gates: float32 [8192, 2], P('expert'), may hold values from 0.2 to 0.8
- w_gate: bfloat16 [64, 2048, 1408], P('expert', None, 'mp'), may hold values from -0.125 to 0.125
- w_up: bfloat16 [64, 2048, 1408], P('expert', None, 'mp'), may hold values from -0.125 to 0.125
- w_down: bfloat16 [64, 1408, 2048], P('expert', 'mp'), may hold values from -0.15625 to 0.15625
Outputs:
- hvp: float32 [4, 512, 2048], P('mp', 'expert')
Inputs may be any that keep to these rules, and one draw needn't show every extreme that they name: `routes`: in each group of 128 rows held along one index of expert, no expert is named by more than 5 rows, a bound that some block reaches; the two experts of a row differ.
All inputs are finite; a program needn't handle non-finite values.
Results may differ from a plain program's by a relative error of at most 0.03.
Values may be sent and summed in bfloat16 or wider, within the bound.
A program may use at most 128 MiB of HBM per device.

v0:
```python
import math

import jax
import jax.numpy as jnp
from jax import lax
from jax.sharding import PartitionSpec as P


def silu_terms(gate_pre):
    sigma = jax.nn.sigmoid(gate_pre)
    silu_val = gate_pre * sigma
    silu_one = sigma * (1.0 + gate_pre * (1.0 - sigma))
    silu_two = sigma * (1.0 - sigma) * (2.0 + gate_pre * (1.0 - 2.0 * sigma))
    return (silu_val, silu_one, silu_two)


def pre_acts(inputs, inputs_tan, gate_w, up_w):
    gate_pre = jnp.dot(inputs, gate_w, preferred_element_type=jnp.float32)
    up_pre = jnp.dot(inputs, up_w, preferred_element_type=jnp.float32)
    gate_tan = jnp.dot(inputs_tan, gate_w, preferred_element_type=jnp.float32)
    up_tan = jnp.dot(inputs_tan, up_w, preferred_element_type=jnp.float32)
    return (gate_pre, up_pre, gate_tan, up_tan)


def contract_last(left, right):
    return lax.dot_general(
        left, right, (((1,), (1,)), ((), ())), preferred_element_type=jnp.float32
    )


def route_slots(routes, gates, experts, capacity):
    flat_ids = routes.reshape(-1)
    count = flat_ids.shape[0]
    onehot = (flat_ids[:, None] == jnp.arange(experts, dtype=jnp.int32)[None, :]).astype(jnp.int32)
    position = jnp.sum(jnp.cumsum(onehot, axis=0) * onehot, axis=1) - 1
    slot_index = flat_ids * capacity + position
    numbers = jnp.arange(count, dtype=jnp.int32)
    source = jnp.zeros((experts * capacity,), jnp.int32).at[slot_index].set(numbers // 2)
    filled = jnp.zeros((experts * capacity,), jnp.bool_).at[slot_index].set(True)
    slot_gate = jnp.zeros((experts * capacity,), jnp.float32).at[slot_index].set(gates.reshape(-1))
    return (slot_index, source, filled, slot_gate)


def local(attn, out_proj, tangent_proj, resid, target, routes, gates, w_gate, w_up, w_down):
    expert_count = lax.axis_size("expert")
    group_rows = attn.shape[0]
    quarter = attn.shape[1]
    model_width = out_proj.shape[1]
    experts = expert_count * w_gate.shape[0]
    capacity = max(2, 5 * 2 * group_rows // (4 * experts))
    z_term = jnp.dot(attn, out_proj, preferred_element_type=jnp.float32)
    z_tan_term = jnp.dot(attn, tangent_proj, preferred_element_type=jnp.float32)
    z_val, z_tan = (
        lax.psum_scatter(z_term.astype(jnp.bfloat16), "mp", scatter_dimension=1, tiled=True).astype(
            jnp.float32
        ),
        lax.psum_scatter(
            z_tan_term.astype(jnp.bfloat16), "mp", scatter_dimension=1, tiled=True
        ).astype(jnp.float32),
    )
    x_part = (resid.astype(jnp.float32) + z_val).astype(jnp.bfloat16)
    x_tan_part = z_tan.astype(jnp.bfloat16)
    slot_index, source, filled, slot_gate = route_slots(routes, gates, experts, capacity)

    def spread(values):
        taken = jnp.where(filled[:, None], values[source], jnp.zeros((), values.dtype))
        return taken.reshape(experts, capacity, values.shape[1])

    def weighted(values):
        taken = (slot_gate[:, None] * values[source]).astype(jnp.bfloat16)
        return taken.reshape(experts, capacity, values.shape[1])

    def combine(values):
        picked = values.reshape(experts * capacity, quarter)[slot_index].astype(jnp.float32)
        picked = picked.reshape(group_rows, 2, quarter)
        return jnp.sum(gates[:, :, None] * picked, axis=1)

    x_full, x_tan_full = (
        lax.all_gather(x_part, "mp", axis=1, tiled=True),
        lax.all_gather(x_tan_part, "mp", axis=1, tiled=True),
    )
    inputs, inputs_tan = (
        lax.all_to_all(spread(x_full), "expert", split_axis=0, concat_axis=0, tiled=True),
        lax.all_to_all(spread(x_tan_full), "expert", split_axis=0, concat_axis=0, tiled=True),
    )
    inputs = inputs.reshape(-1, model_width)
    inputs_tan = inputs_tan.reshape(-1, model_width)
    gate_w = w_gate[0]
    up_w = w_up[0]
    down_w = w_down[0]
    gate_pre, up_pre, gate_tan, up_tan = pre_acts(inputs, inputs_tan, gate_w, up_w)
    silu_val, silu_one, silu_two = silu_terms(gate_pre)
    hidden = (silu_val * up_pre).astype(jnp.bfloat16)
    hidden_tan = (silu_one * gate_tan * up_pre + silu_val * up_tan).astype(jnp.bfloat16)
    out_part = jnp.dot(hidden, down_w, preferred_element_type=jnp.float32)
    out_tan_part = jnp.dot(hidden_tan, down_w, preferred_element_type=jnp.float32)
    out_row, out_tan = (
        lax.psum_scatter(
            out_part.astype(jnp.bfloat16), "mp", scatter_dimension=1, tiled=True
        ).astype(jnp.float32),
        lax.psum_scatter(
            out_tan_part.astype(jnp.bfloat16), "mp", scatter_dimension=1, tiled=True
        ).astype(jnp.float32),
    )
    out_row = out_row.astype(jnp.bfloat16).reshape(expert_count, capacity, quarter)
    out_tan = out_tan.astype(jnp.bfloat16).reshape(expert_count, capacity, quarter)
    back_row, back_tan_row = (
        lax.all_to_all(out_row, "expert", split_axis=0, concat_axis=0, tiled=True),
        lax.all_to_all(out_tan, "expert", split_axis=0, concat_axis=0, tiled=True),
    )
    y_val = x_part.astype(jnp.float32) + combine(back_row)
    y_tan = x_tan_part.astype(jnp.float32) + combine(back_tan_row)
    diff = y_val - target.astype(jnp.float32)
    diff_full, y_tan_full = (
        lax.all_gather(diff.astype(jnp.bfloat16), "mp", axis=1, tiled=True).astype(diff.dtype),
        lax.all_gather(y_tan.astype(jnp.bfloat16), "mp", axis=1, tiled=True).astype(y_tan.dtype),
    )
    cot, cot_tan = (
        lax.all_to_all(weighted(diff_full), "expert", split_axis=0, concat_axis=0, tiled=True),
        lax.all_to_all(weighted(y_tan_full), "expert", split_axis=0, concat_axis=0, tiled=True),
    )
    cot = cot.reshape(-1, model_width)
    cot_tan = cot_tan.reshape(-1, model_width)
    grad_h = contract_last(cot, down_w)
    grad_h_tan = contract_last(cot_tan, down_w)
    da_tan = (
        (grad_h_tan * up_pre + grad_h * up_tan) * silu_one + grad_h * up_pre * silu_two * gate_tan
    ).astype(jnp.bfloat16)
    db_tan = (grad_h_tan * silu_val + grad_h * silu_one * gate_tan).astype(jnp.bfloat16)
    back_part = contract_last(da_tan, gate_w) + contract_last(db_tan, up_w)
    back_sum = lax.psum_scatter(
        back_part.astype(jnp.bfloat16), "mp", scatter_dimension=1, tiled=True
    ).astype(jnp.float32)
    back_sum = back_sum.astype(jnp.bfloat16).reshape(expert_count, capacity, quarter)
    back_home = lax.all_to_all(back_sum, "expert", split_axis=0, concat_axis=0, tiled=True)
    dx_tan = (y_tan + combine(back_home)).astype(jnp.bfloat16)
    dx_full = lax.all_gather(dx_tan, "mp", axis=1, tiled=True)
    inv_root = 1.0 / math.sqrt(group_rows * expert_count)
    product = lax.dot_general(
        attn, dx_full, (((0,), (0,)), ((), ())), preferred_element_type=jnp.float32
    )
    hvp_rows = lax.psum_scatter(product * inv_root, "expert", scatter_dimension=0, tiled=True)
    return hvp_rows[None]


def solution(mesh):
    in_specs = (
        P("expert", "mp"),
        P("mp", None),
        P("mp", None),
        P("expert", "mp"),
        P("expert", "mp"),
        P("expert", None),
        P("expert", None),
        P("expert", None, "mp"),
        P("expert", None, "mp"),
        P("expert", "mp", None),
    )
    out_specs = P("mp", "expert", None)
    return jax.shard_map(local, mesh=mesh, in_specs=in_specs, out_specs=out_specs, check_vma=False)
```

profile of v0, /device:TPU:1, one launch (start us, length us, event | category | flops | bytes accessed | tf_op | source)
XLA Modules:
  0.0 734.2 jit_solution(2708000165280387869)
XLA Ops:
  10.4 2.8 convolution_convert_fusion.2
  18.0 18.5 %reduce-scatter.7.cloned.1.call-done = bf16[128,512]{1,0:T(8,128)(2,1)} async-done(((bf16[128,2048]{1,0:T(8,128)(2,1)}), bf16[128,512]{1,0:T(8,128)(2,1)}) %reduce-scatter.7.cloned.1.call-update) | async-done | bytes 131088 | tf_op jit(solution)/shard_map/reduce_scatter | solution.py:57
  36.5 11.3 %all_gather.16 = bf16[128,2048]{1,0:T(8,128)(2,1)S(1)} all-gather(bf16[128,512]{1,0:T(8,128)(2,1)} %reduce-scatter.7.cloned.1.call-done), channel_id=1, replica_groups=mesh['expert'=64,'mp'=4] {'mp'}, dimensions={1}, use_global_device_ids=true | all-gather | bytes 655360 | tf_op jit(solution)/shard_map/all_gather | solution.py:80
  51.9 10.9 %reduce-scatter.9.cloned.1.call-done = bf16[128,512]{1,0:T(8,128)(2,1)} async-done(((bf16[128,2048]{1,0:T(8,128)(2,1)}), bf16[128,512]{1,0:T(8,128)(2,1)}) %reduce-scatter.9.cloned.1.call-update) | async-done | bytes 131088 | tf_op jit(solution)/shard_map/reduce_scatter | solution.py:54
  63.7 11.1 %all_gather.15 = bf16[128,2048]{1,0:T(8,128)(2,1)S(1)} all-gather(bf16[128,512]{1,0:T(8,128)(2,1)S(1)} %add_convert_fusion.3), channel_id=1, replica_groups=mesh['expert'=64,'mp'=4] {'mp'}, dimensions={1}, use_global_device_ids=true | all-gather | bytes 655360 | tf_op jit(solution)/shard_map/all_gather | solution.py:79
  78.8 4.0 broadcast_select_fusion.1
  82.8 63.7 %all_to_all.35 = bf16[64,5,2048]{2,1,0:T(8,128)(2,1)} all-to-all(bf16[64,5,2048]{2,1,0:T(8,128)(2,1)S(1)} %get-tuple-element.9), channel_id=1, replica_groups=mesh['expert'=64,'mp'=4] {'expert'}, dimensions={0} | all-to-all | bytes 2621440 | tf_op jit(solution)/shard_map/all_to_all | solution.py:83
  146.5 7.0 all-to-all-start.1
  153.7 3.6 reshape.126
  161.8 41.4 %all-to-all-done.1 = bf16[64,5,2048]{2,1,0:T(8,128)(2,1)S(1)} async-done(((bf16[64,5,2048]{2,1,0:T(8,128)(2,1)}), bf16[64,5,2048]{2,1,0:T(8,128)(2,1)S(1)}, u32[]{:S(2)}, u32[]{:S(2)}) %all-to-all-start.1) | async-done | bytes 1310752 | tf_op jit(solution)/shard_map/all_to_all | solution.py:84
  213.2 19.9 %reduce-scatter.11.cloned.1.call-done = bf16[320,512]{1,0:T(8,128)(2,1)} async-done(((bf16[320,2048]{1,0:T(8,128)(2,1)}), bf16[320,512]{1,0:T(8,128)(2,1)}) %reduce-scatter.11.cloned.1.call-update) | async-done | bytes 327696 | tf_op jit(solution)/shard_map/reduce_scatter | solution.py:101
  235.0 12.1 %all-to-all-start.2 = ((bf16[64,5,512]{2,1,0:T(8,128)(2,1)}), bf16[64,5,512]{2,1,0:T(8,128)(2,1)S(1)}, u32[]{:S(2)}, u32[]{:S(2)}) async-start(bf16[64,5,512]{2,1,0:T(8,128)(2,1)} %reshape.128), calls=%async_computation.5 | async-start | bytes 1048576 | tf_op jit(solution)/shard_map/all_to_all | solution.py:109
  247.1 15.3 %reduce-scatter.13.cloned.1.call-done = bf16[320,512]{1,0:T(8,128)(2,1)} async-done(((bf16[320,2048]{1,0:T(8,128)(2,1)}), bf16[320,512]{1,0:T(8,128)(2,1)}) %reduce-scatter.13.cloned.1.call-update) | async-done | bytes 327696 | tf_op jit(solution)/shard_map/reduce_scatter | solution.py:98
  264.8 11.3 %all-to-all-start.4 = ((bf16[64,5,512]{2,1,0:T(8,128)(2,1)}), bf16[64,5,512]{2,1,0:T(8,128)(2,1)S(1)}, u32[]{:S(2)}, u32[]{:S(2)}) async-start(bf16[64,5,512]{2,1,0:T(8,128)(2,1)} %reshape.132), calls=%async_computation.8 | async-start | bytes 1048576 | tf_op jit(solution)/shard_map/all_to_all | solution.py:108
  280.3 13.6 %all-to-all-done.4 = bf16[64,5,512]{2,1,0:T(8,128)(2,1)S(1)} async-done(((bf16[64,5,512]{2,1,0:T(8,128)(2,1)}), bf16[64,5,512]{2,1,0:T(8,128)(2,1)S(1)}, u32[]{:S(2)}, u32[]{:S(2)}) %all-to-all-start.4) | async-done | bytes 327712 | tf_op jit(solution)/shard_map/all_to_all | solution.py:108
  297.0 10.1 %all_gather.18 = bf16[128,2048]{1,0:T(8,128)(2,1)S(1)} all-gather(bf16[128,512]{1,0:T(8,128)(2,1)S(1)} %subtract_convert_fusion), channel_id=1, replica_groups=mesh['expert'=64,'mp'=4] {'mp'}, dimensions={1}, use_global_device_ids=true | all-gather | bytes 655360 | tf_op jit(solution)/shard_map/all_gather | solution.py:115
  307.2 3.1 gather_fusion.5
  310.3 4.1 gather.38
  314.5 9.9 %all_gather.17 = bf16[128,2048]{1,0:T(8,128)(2,1)S(1)} all-gather(bf16[128,512]{1,0:T(8,128)(2,1)S(1)} %fusion.29), channel_id=1, replica_groups=mesh['expert'=64,'mp'=4] {'mp'}, dimensions={1}, use_global_device_ids=true | all-gather | bytes 655360 | tf_op jit(solution)/shard_map/all_gather | solution.py:116
  324.5 3.1 gather_fusion.3
  327.6 4.1 gather.35
  331.7 6.1 multiply_convert_fusion.1
  337.8 62.4 %all_to_all.36 = bf16[64,5,2048]{2,1,0:T(8,128)(2,1)} all-to-all(bf16[64,5,2048]{2,1,0:T(8,128)(2,1)S(1)} %get-tuple-element.8), channel_id=1, replica_groups=mesh['expert'=64,'mp'=4] {'expert'}, dimensions={0} | all-to-all | bytes 2621440 | tf_op jit(solution)/shard_map/all_to_all | solution.py:119
  400.3 7.0 all-to-all-start.3
  407.3 3.6 reshape.134
  411.0 3.4 fusion.1
  414.4 42.6 %all-to-all-done.3 = bf16[64,5,2048]{2,1,0:T(8,128)(2,1)S(1)} async-done(((bf16[64,5,2048]{2,1,0:T(8,128)(2,1)}), bf16[64,5,2048]{2,1,0:T(8,128)(2,1)S(1)}, u32[]{:S(2)}, u32[]{:S(2)}) %all-to-all-start.3) | async-done | bytes 1310752 | tf_op jit(solution)/shard_map/all_to_all | solution.py:120
  458.4 2.8 fusion.4
  464.7 21.9 %reduce-scatter.15.cloned.1.call-done = bf16[320,512]{1,0:T(8,128)(2,1)} async-done(((bf16[320,2048]{1,0:T(8,128)(2,1)}), bf16[320,512]{1,0:T(8,128)(2,1)}) %reduce-scatter.15.cloned.1.call-update) | async-done | bytes 327696 | tf_op jit(solution)/shard_map/reduce_scatter | solution.py:131
  487.8 29.5 %all_to_all.37 = bf16[64,5,512]{2,1,0:T(8,128)(2,1)S(1)} all-to-all(bf16[64,5,512]{2,1,0:T(8,128)(2,1)S(1)} %reshape.135), channel_id=1, replica_groups=mesh['expert'=64,'mp'=4] {'expert'}, dimensions={0} | all-to-all | bytes 655360 | tf_op jit(solution)/shard_map/all_to_all | solution.py:135
  519.7 9.9 %all_gather.19 = bf16[128,2048]{1,0:T(8,128)(2,1)S(1)} all-gather(bf16[128,512]{1,0:T(8,128)(2,1)S(1)} %add_convert_fusion.2), channel_id=1, replica_groups=mesh['expert'=64,'mp'=4] {'mp'}, dimensions={1}, use_global_device_ids=true | all-gather | bytes 655360 | tf_op jit(solution)/shard_map/all_gather | solution.py:137
  534.4 190.5 %all-reduce.3.cloned.1.call-done = f32[512,2048]{0,1:T(8,128)} async-done(((f32[512,2048]{0,1:T(8,128)}), f32[512,2048]{0,1:T(8,128)}) %all-reduce.3.cloned.1.call-update) | async-done | bytes 4194320
  (124 shorter events, 58.6 us)
Async XLA Ops:
  6.5 1.6 copy-start
  6.5 3.8 copy-start.10
  6.5 30.0 %reduce-scatter.7.cloned.1.call-start = ((), (), s32[]{:S(2)}) async-start(), calls=%async_computation.12 | async-start | bytes 655360 | tf_op jit(solution)/shard_map/reduce_scatter | solution.py:57
  10.3 2.9 copy-start.18
  10.3 52.5 %reduce-scatter.9.cloned.1.call-start = ((), (), s32[]{:S(2)}) async-start(), calls=%async_computation.13 | async-start | bytes 655360 | tf_op jit(solution)/shard_map/reduce_scatter | solution.py:54
  50.2 12.6 %copy-start.16 = (bf16[128,512]{1,0:T(8,128)(2,1)S(1)}, bf16[128,512]{1,0:T(8,128)(2,1)}, u32[]{:S(2)}) copy-start(bf16[128,512]{1,0:T(8,128)(2,1)} %param.13) | copy-start | bytes 393220
  146.5 56.7 %all-to-all-start.1 = ((bf16[64,5,2048]{2,1,0:T(8,128)(2,1)}), bf16[64,5,2048]{2,1,0:T(8,128)(2,1)S(1)}, u32[]{:S(2)}, u32[]{:S(2)}) async-start(bf16[64,5,2048]{2,1,0:T(8,128)(2,1)} %get-tuple-element.10), calls=%async_computation.3 | async-start | bytes 4194304 | tf_op jit(solution)/shard_map/all_to_all | solution.py:84
  153.5 79.6 %reduce-scatter.11.cloned.1.call-start = ((), (), s32[]{:S(2)}) async-start(), calls=%async_computation.14 | async-start | bytes 1638400 | tf_op jit(solution)/shard_map/reduce_scatter | solution.py:101
  157.3 2.8 copy-start.3
  157.4 2.8 copy-start.7
  204.6 2.8 copy-start.4
  204.6 2.8 copy-start.8
  207.3 1.7 copy-start.12
  207.3 1.7 copy-start.20
  208.2 0.8 copy-start.14
  209.0 2.2 copy-start.21
  211.1 51.3 %reduce-scatter.13.cloned.1.call-start = ((), (), s32[]{:S(2)}) async-start(), calls=%async_computation.15 | async-start | bytes 1638400 | tf_op jit(solution)/shard_map/reduce_scatter | solution.py:98
  235.0 41.2 %copy-start.19 = (f32[128,2]{0,1:T(2,128)S(1)}, f32[128,2]{0,1:T(2,128)}, u32[]{:S(2)}) copy-start(f32[128,2]{0,1:T(2,128)} %param.16) | copy-start | bytes 3076
  235.0 29.8 %all-to-all-start.2 = ((bf16[64,5,512]{2,1,0:T(8,128)(2,1)}), bf16[64,5,512]{2,1,0:T(8,128)(2,1)S(1)}, u32[]{:S(2)}, u32[]{:S(2)}) async-start(bf16[64,5,512]{2,1,0:T(8,128)(2,1)} %reshape.128), calls=%async_computation.5 | async-start | bytes 1048576 | tf_op jit(solution)/shard_map/all_to_all | solution.py:109
  264.8 29.1 %all-to-all-start.4 = ((bf16[64,5,512]{2,1,0:T(8,128)(2,1)}), bf16[64,5,512]{2,1,0:T(8,128)(2,1)S(1)}, u32[]{:S(2)}, u32[]{:S(2)}) async-start(bf16[64,5,512]{2,1,0:T(8,128)(2,1)} %reshape.132), calls=%async_computation.8 | async-start | bytes 1048576 | tf_op jit(solution)/shard_map/all_to_all | solution.py:108
  295.2 1.7 copy-start.17
  310.3 4.1 copy-start.9
  400.3 56.7 %all-to-all-start.3 = ((bf16[64,5,2048]{2,1,0:T(8,128)(2,1)}), bf16[64,5,2048]{2,1,0:T(8,128)(2,1)S(1)}, u32[]{:S(2)}, u32[]{:S(2)}) async-start(bf16[64,5,2048]{2,1,0:T(8,128)(2,1)} %get-tuple-element.7), calls=%async_computation.6 | async-start | bytes 4194304 | tf_op jit(solution)/shard_map/all_to_all | solution.py:120
  407.3 79.4 %reduce-scatter.15.cloned.1.call-start = ((), (), s32[]{:S(2)}) async-start(), calls=%async_computation.16 | async-start | bytes 1638400 | tf_op jit(solution)/shard_map/reduce_scatter | solution.py:131
  458.3 2.8 copy-start.2
  458.4 2.8 copy-start.6
  458.4 2.8 copy-start.13
  458.4 2.8 copy-start.15
  461.2 1.4 copy-start.5
  464.7 260.2 %all-reduce.3.cloned.1.call-start = ((), (), s32[]{:S(2)}) async-start(), calls=%async_computation.17 | async-start | bytes 8388608
  518.6 11.0 %copy-start.11 = (bf16[128,512]{1,0:T(8,128)(2,1)S(1)}, bf16[128,512]{1,0:T(8,128)(2,1)}, u32[]{:S(2)}) copy-start(bf16[128,512]{1,0:T(8,128)(2,1)} %param.10) | copy-start | bytes 393220
  533.6 193.8 %copy-start.1 = (bf16[512,2048]{1,0:T(8,128)(2,1)S(1)}, bf16[512,2048]{1,0:T(8,128)(2,1)}, u32[]{:S(2)}) copy-start(bf16[512,2048]{1,0:T(8,128)(2,1)} %param.12) | copy-start | bytes 6291460
  (1 other events, 0.7 us)
Sparse Core Ops, SparseCore 0:
  10.4 26.0 reduce-scatter.6
  39.1 23.7 reduce-scatter.8
  211.3 21.7 reduce-scatter.10
  235.5 26.8 reduce-scatter.12
  464.8 21.8 reduce-scatter.14
  532.4 192.3 all-reduce.2
where the time goes:
time: 736 us; the launch traced here: 734 us
  waiting for transfers between devices  375 us (51%)
  blocking collectives  208 us (28%)
  local copies, waits for them, and re-layouts  55.1 us (7%)
  starting transfers between devices  37.9 us (5%)
  matrix products  29.1 us (4%)
  between operations  14.7 us (2%)
  other arithmetic  14.2 us (2%)
    unnamed x7, waiting for transfers between devices  191 us
    all_to_all x1, blocking collectives, local(): lax.all_to_all(spread(x_full), 'expert', split_axis=0, concat_axis=0, til...  63.7 us
    all_to_all x1, blocking collectives, local(): lax.all_to_all(weighted(diff_full), 'expert', split_axis=0, concat_axis=0...  62.4 us
    all_to_all x1, waiting for transfers between devices, local(): lax.all_to_all(weighted(y_tan_full), 'expert', split_axis=0, concat_axis=...  42.6 us
    all_to_all x1, waiting for transfers between devices, local(): lax.all_to_all(spread(x_tan_full), 'expert', split_axis=0, concat_axis=0,...  41.4 us
    all_to_all x1, blocking collectives, local(): lax.all_to_all(back_sum, 'expert', split_axis=0, concat_axis=0, tiled=True)  29.5 us
    reduce_scatter x1, waiting for transfers between devices, local(): lax.psum_scatter(back_part.astype(jnp.bfloat16), 'mp', scatter_dimension=...  21.9 us
    reduce_scatter x1, waiting for transfers between devices, local(): lax.psum_scatter(out_tan_part.astype(jnp.bfloat16), 'mp', scatter_dimensi...  19.9 us
  transfers between devices with their start and end apart: 10, of which 10 were waited for; matrix products, arithmetic and copies ran while one was open for 5% of the time, Pallas kernels for 0%

commit v1 on v0

v1 whole, which is shorter than its diff:
```python
import functools
import math

import jax
import jax.numpy as jnp
from jax import lax
from jax.experimental import pallas as pl
from jax.experimental.pallas import tpu as pltpu
from jax.sharding import PartitionSpec as P

MESH = pl.DeviceIdType.MESH
BF = jnp.bfloat16
F32 = jnp.float32
N_MP = 4
N_CORE = 2
CHUNKS = 2
BACK_CHUNKS = 2


class Names:
    def __init__(self):
        self.names, self.shapes = [], []

    def add(self, name, shape):
        self.names.append(name)
        self.shapes.append(shape)

    def bind(self, refs):
        for name, ref in zip(self.names, refs, strict=True):
            setattr(self, name, ref)


def dot(left, right):
    return jnp.dot(left, right, preferred_element_type=F32)


def dot_last(left, right):
    return lax.dot_general(left, right, (((1,), (1,)), ((), ())), preferred_element_type=F32)


def dot_first(left, right):
    return lax.dot_general(left, right, (((0,), (0,)), ((), ())), preferred_element_type=F32)


def silu_terms(gate_pre):
    sigma = jax.nn.sigmoid(gate_pre)
    silu_val = gate_pre * sigma
    silu_one = sigma * (1.0 + gate_pre * (1.0 - sigma))
    silu_two = sigma * (1.0 - sigma) * (2.0 + gate_pre * (1.0 - 2.0 * sigma))
    return (silu_val, silu_one, silu_two)


def each(lower, upper, body):
    def step(i, carry):
        body(i)
        return carry

    lax.fori_loop(lower, upper, step, 0)


def pipeline(stages, chunks):
    for turn in range(len(stages) + chunks - 1):
        for k in range(chunks):
            if 0 <= turn - k < len(stages):
                stages[turn - k](k)


class Exchange:
    def __init__(self, src, dst, sems, n, me, device):
        self.src, self.dst, self.n, self.me, self.device = src, dst, n, me, device
        self.ssem, self.rsem = sems

    def copy(self, k, d, block, landing, device):
        return pltpu.make_async_remote_copy(
            src_ref=self.src.at[k, block],
            dst_ref=self.dst.at[k, landing],
            send_sem=self.ssem.at[k, d],
            recv_sem=self.rsem.at[k, d],
            device_id=device,
            device_id_type=MESH,
        )

    def out(self, k, d):
        to = lax.rem(self.me + d, self.n)
        return self.copy(k, d, to, self.me, self.device(to))

    def start(self, k):
        each(1, self.n, lambda d: self.out(k, d).start())
        self.dst[k, pl.ds(self.me, 1)] = self.src[k, pl.ds(self.me, 1)]

    def wait(self, k):
        def body(d):
            source = lax.rem(self.me + self.n - d, self.n)
            self.copy(k, d, source, source, self.device(source)).wait_recv()

        each(1, self.n, body)

    def drain(self, k):
        each(1, self.n, lambda d: self.out(k, d).wait_send())


class Ring:
    def __init__(self):
        self.expert = lax.axis_index("expert")
        self.me = lax.axis_index("mp")
        self.right = lax.rem(self.me + 1, N_MP)
        self.left = lax.rem(self.me + N_MP - 1, N_MP)
        self.opp = lax.rem(self.me + 2, N_MP)

    def copy(self, src, dst, ssem, rsem, to):
        return pltpu.make_async_remote_copy(
            src_ref=src,
            dst_ref=dst,
            send_sem=ssem,
            recv_sem=rsem,
            device_id=(self.expert, to),
            device_id_type=MESH,
        )


class Scatter:
    def __init__(self, ring, part, hop, total, sems, rows):
        self.ring, self.part, self.hop, self.total, self.rows = ring, part, hop, total, rows
        self.ssem, self.rsem = sems
        self.half = rows // 2

    def copy(self, k, i):
        r, h = self.ring, self.half
        first, second = pl.ds(0, h), pl.ds(h, h)
        part, hop, total = self.part.at[k], self.hop.at[k], self.total.at[k]
        plan = (
            (part.at[r.opp, first], hop.at[0], r.left),
            (part.at[r.opp, second], hop.at[1], r.right),
            (part.at[r.left, second], total.at[0, second], r.left),
            (part.at[r.right, first], total.at[1, first], r.right),
            (part.at[r.left, first], total.at[0, first], r.left),
            (part.at[r.right, second], total.at[1, second], r.right),
        )
        src, dst, to = plan[i]
        return r.copy(src, dst, self.ssem.at[k, i], self.rsem.at[k, i], to)

    def start(self, k, index):
        self.copy(k, index).start()

    def middle(self, k):
        r, h = self.ring, self.half
        self.copy(k, 0).wait_recv()
        self.add(k, r.left, pl.ds(0, h), 0)
        self.copy(k, 4).start()
        self.copy(k, 1).wait_recv()
        self.add(k, r.right, pl.ds(h, h), 1)
        self.copy(k, 5).start()

    def add(self, k, block, rows, side):
        value = self.part[k, pl.ds(block, 1), rows, :][0].astype(F32) + self.hop[k, side].astype(F32)
        self.part[k, pl.ds(block, 1), rows, :] = value.astype(BF)[None]

    def finish(self, k):
        for i in (2, 3, 4, 5):
            self.copy(k, i).wait_recv()
        own = self.part[k, pl.ds(self.ring.me, 1)][0].astype(F32)
        return own + self.total[k, 0].astype(F32) + self.total[k, 1].astype(F32)

    def drain(self, k):
        for i in range(6):
            self.copy(k, i).wait_send()


class Gather:
    def __init__(self, ring, full, sems, rows):
        self.ring, self.full = ring, full
        self.ssem, self.rsem = sems
        self.half = rows // 2

    def move(self, k, i, block, rows, to):
        ref = self.full.at[k, block, rows]
        return self.ring.copy(ref, ref, self.ssem.at[k, i], self.rsem.at[k, i], to)

    def copy(self, k, i):
        r, h = self.ring, self.half
        first, second = pl.ds(0, h), pl.ds(h, h)
        plan = (
            (r.me, first, r.left),
            (r.me, second, r.right),
            (r.me, second, r.left),
            (r.me, first, r.right),
            (r.right, first, r.left),
            (r.left, second, r.right),
        )
        return self.move(k, i, *plan[i])

    def arrival(self, k, i):
        r, h = self.ring, self.half
        first, second = pl.ds(0, h), pl.ds(h, h)
        plan = (
            (r.right, first),
            (r.left, second),
            (r.right, second),
            (r.left, first),
            (r.opp, first),
            (r.opp, second),
        )
        return self.move(k, i, *plan[i], r.left)

    def start(self, k):
        for i in range(4):
            self.copy(k, i).start()

    def middle(self, k):
        for i in range(2):
            self.arrival(k, i).wait_recv()
            self.copy(k, 4 + i).start()

    def finish(self, k):
        for i in range(2, 6):
            self.arrival(k, i).wait_recv()

    def drain(self, k):
        for i in range(6):
            self.copy(k, i).wait_send()


def iota(shape, dim):
    return lax.broadcasted_iota(jnp.int32, shape, dim)


def kernel(sizes, names, *refs):
    (attn_h, out_proj_h, tan_proj_h, resid, target, pick, back0, back1, slot_gate, gates) = refs[:10]
    w_gate_h, w_up_h, w_down_h, out = refs[10:14]
    s = names
    s.bind(refs[14:])
    nz, nyc, cap, tokens, quarter, hidden, chunks, back_chunks = sizes
    ny = nyc // N_CORE
    cw = quarter // chunks
    bw = quarter // 2 // back_chunks
    half = nz * cap
    block = 2 * half
    rows = nyc * block
    model = N_MP * quarter

    ring = Ring()
    me_e, me_m = ring.expert, ring.me
    z, yc = lax.div(me_e, nyc), lax.rem(me_e, nyc)
    y, core = lax.div(yc, N_CORE), lax.rem(yc, N_CORE)

    def at_z(to):
        return (to * nyc + yc, me_m)

    def at_yc(to):
        return (z * nyc + to, me_m)

    loads = [
        pltpu.make_async_copy(src, dst, s.load_sem.at[i])
        for i, (src, dst) in enumerate(
            (
                (attn_h, s.attn),
                (out_proj_h, s.out_proj),
                (tan_proj_h, s.tan_proj),
                (w_gate_h.at[0], s.w_gate),
                (w_up_h.at[0], s.w_up),
                (w_down_h.at[0], s.w_down),
            )
        )
    ]
    for load in loads:
        load.start()

    barrier = pltpu.get_barrier_semaphore()

    def greet(device):
        pl.semaphore_signal(barrier, inc=1, device_id=device, device_id_type=MESH)

    each(1, nz, lambda d: greet(at_z(lax.rem(z + d, nz))))
    each(1, nyc, lambda d: greet(at_yc(lax.rem(yc + d, nyc))))
    each(1, N_MP, lambda d: greet((me_e, lax.rem(me_m + d, N_MP))))
    pl.semaphore_wait(barrier, nz + nyc + N_MP - 3)

    def sems(name):
        return getattr(s, name + "_ssem"), getattr(s, name + "_rsem")

    scat_z = Scatter(ring, s.part_z, s.hop_z, s.total_z, sems("scat_z"), 2 * tokens)
    go_z = Exchange(s.go_a, s.go_b, sems("go_z"), nz, z, at_z)
    go_yc = Exchange(s.go_c, s.go_d, sems("go_yc"), nyc, yc, at_yc)
    gather_x = Gather(ring, s.x_full, sems("gather_x"), rows)
    scat_o = Scatter(ring, s.part_o, s.hop_o, s.total_o, sems("scat_o"), rows)
    ret_yc = Exchange(s.ret_a, s.ret_b, sems("ret_yc"), nyc, yc, at_yc)
    ret_z = Exchange(s.ret_c, s.ret_d, sems("ret_z"), nz, z, at_z)
    cot_z = Exchange(s.cot_a, s.cot_b, sems("cot_z"), nz, z, at_z)
    cot_yc = Exchange(s.cot_c, s.cot_d, sems("cot_yc"), nyc, yc, at_yc)
    gather_c = Gather(ring, s.c_full, sems("gather_c"), rows)
    scat_b = Scatter(ring, s.part_b, s.hop_b, s.total_b, sems("scat_b"), rows)
    bak_yc = Exchange(s.bak_a, s.bak_b, sems("bak_yc"), nyc, yc, at_yc)
    bak_z = Exchange(s.bak_c, s.bak_d, sems("bak_z"), nz, z, at_z)
    gather_a = Gather(ring, s.attn_full, sems("gather_a"), tokens)

    def swap(src, dst, k, width):
        value = dot(s.swap[...], src[k].reshape(rows, width))
        dst[k] = value.astype(BF).reshape(nyc, block, width)

    loads[0].wait()
    loads[1].wait()
    loads[2].wait()

    def z_part(k, q):
        columns = pl.ds(pl.multiple_of(q * quarter + k * cw, 128), cw)
        s.part_z[k, pl.ds(q, 1), pl.ds(0, tokens), :] = dot(s.attn[...], s.out_proj[:, columns]).astype(BF)[None]
        s.part_z[k, pl.ds(q, 1), pl.ds(tokens, tokens), :] = dot(s.attn[...], s.tan_proj[:, columns]).astype(BF)[None]

    def z_start(k):
        z_part(k, ring.opp)
        scat_z.start(k, 0)
        scat_z.start(k, 1)
        z_part(k, ring.left)
        scat_z.start(k, 2)
        z_part(k, ring.right)
        scat_z.start(k, 3)
        z_part(k, ring.me)

    def spread_x(k):
        if k == 0:
            r = iota((rows, 1), 0)
            a, h, b, p = r // block, (r % block) // half, (r % half) // cap, r % cap
            s.swap[...] = (iota((rows, rows), 1) == b * block + h * half + a * cap + p).astype(F32).astype(BF)
        value = scat_z.finish(k)
        columns = pl.ds(k * cw, cw)
        s.x_in[k, pl.ds(0, tokens), :] = (
            resid[:, columns].astype(F32) + value[:tokens]
        ).astype(BF)
        s.x_in[k, pl.ds(tokens, tokens), :] = value[tokens:].astype(BF)
        s.go_a[k] = dot(pick[...], s.x_in[k]).astype(BF).reshape(nz, block, cw)
        go_z.start(k)

    def pass_x(k):
        go_z.wait(k)
        swap(s.go_b, s.go_c, k, cw)
        go_yc.start(k)

    def gather_start_x(k):
        go_yc.wait(k)
        s.x_full[k, pl.ds(me_m, 1)] = s.go_d[k].reshape(1, rows, cw)
        gather_x.start(k)

    step_rows = 2 * block

    def pre_acts(k):
        gather_x.finish(k)
        if k == 0:
            loads[3].wait()
            loads[4].wait()

        def body(i):
            at = pl.ds(pl.multiple_of(i * step_rows, step_rows), step_rows)
            gate = jnp.zeros((step_rows, hidden), F32)
            up = jnp.zeros((step_rows, hidden), F32)
            for m in range(N_MP):
                features = pl.ds(m * quarter + k * cw, cw)
                values = s.x_full[k, m, at, :]
                gate = gate + dot(values, s.w_gate[features, :])
                up = up + dot(values, s.w_up[features, :])
            if k:
                gate = gate + s.gate[at, :]
                up = up + s.up[at, :]
            s.gate[at, :] = gate
            s.up[at, :] = up

        each(0, rows // step_rows, body)

    def permute_attn():
        r = iota((1, quarter), 1)
        per = quarter // (nz * nyc)
        c, yy, zz, p = (
            r // (quarter // N_CORE),
            (r // (nz * per)) % ny,
            (r // per) % nz,
            r % per,
        )
        wanted = ((zz * ny + yy) * N_CORE + c) * per + p
        permute = (iota((quarter, quarter), 0) == wanted).astype(F32).astype(BF)
        s.attn_full[0, pl.ds(me_m, 1)] = dot(s.attn[...], permute).astype(BF)[None]

    def attn_start(k):
        if k == chunks - 1:
            permute_attn()
            gather_a.start(0)

    pipeline(
        (
            z_start,
            scat_z.middle,
            spread_x,
            attn_start,
            pass_x,
            gather_start_x,
            gather_x.middle,
            pre_acts,
        ),
        chunks,
    )
    gather_a.middle(0)

    def activations(i):
        at, tan_at = pl.ds(pl.multiple_of(i * block, 8), half), pl.ds(pl.multiple_of(i * block + half, 8), half)
        gate_pre, gate_tan = s.gate[at, :], s.gate[tan_at, :]
        up_pre, up_tan = s.up[at, :], s.up[tan_at, :]
        silu_val, silu_one, _ = silu_terms(gate_pre)
        hid = silu_val * up_pre
        hid_tan = silu_one * gate_tan * up_pre + silu_val * up_tan
        s.hidden[pl.ds(pl.multiple_of(i * block, 16), block), :] = jnp.concatenate([hid, hid_tan], 0).astype(BF)

    each(0, nyc, activations)
    loads[5].wait()

    def o_part(k, q):
        columns = pl.ds(pl.multiple_of(q * quarter + k * cw, 128), cw)
        s.part_o[k, pl.ds(q, 1)] = dot(s.hidden[...], s.w_down[:, columns]).astype(BF)[None]

    def o_start(k):
        o_part(k, ring.opp)
        scat_o.start(k, 0)
        scat_o.start(k, 1)
        o_part(k, ring.left)
        scat_o.start(k, 2)
        o_part(k, ring.right)
        scat_o.start(k, 3)
        o_part(k, ring.me)

    def return_o(k):
        s.ret_a[k] = scat_o.finish(k).astype(BF).reshape(nyc, block, cw)
        ret_yc.start(k)

    def pass_o(k):
        ret_yc.wait(k)
        swap(s.ret_b, s.ret_c, k, cw)
        ret_z.start(k)

    def combine(values):
        return gates[:, 0:1] * dot(back0[...], values) + gates[:, 1:2] * dot(back1[...], values)

    def residual(k):
        ret_z.wait(k)
        columns = pl.ds(k * cw, cw)
        both = s.x_in[k].astype(F32) + combine(s.ret_d[k].reshape(rows, cw))
        s.y_tan[:, columns] = both[tokens:]
        diff = both[:tokens] - target[:, columns].astype(F32)
        sent = jnp.concatenate([diff, both[tokens:]], 0).astype(BF)
        s.cot_a[k] = (dot(pick[...], sent) * slot_gate[...]).astype(BF).reshape(nz, block, cw)
        cot_z.start(k)

    def pass_c(k):
        cot_z.wait(k)
        swap(s.cot_b, s.cot_c, k, cw)
        cot_yc.start(k)

    def gather_start_c(k):
        cot_yc.wait(k)
        s.c_full[k, pl.ds(me_m, 1)] = s.cot_d[k].reshape(1, rows, cw)
        gather_c.start(k)

    def grad_hidden(k):
        gather_c.finish(k)

        def body(i):
            at = pl.ds(pl.multiple_of(i * step_rows, step_rows), step_rows)
            grad = jnp.zeros((step_rows, hidden), F32)
            for m in range(N_MP):
                features = pl.ds(m * quarter + k * cw, cw)
                grad = grad + dot_last(s.c_full[k, m, at, :], s.w_down[:, features])
            if k:
                grad = grad + s.grad[at, :]
            s.grad[at, :] = grad

        each(0, rows // step_rows, body)

    pipeline(
        (
            o_start,
            scat_o.middle,
            return_o,
            pass_o,
            residual,
            pass_c,
            gather_start_c,
            gather_c.middle,
            grad_hidden,
        ),
        chunks,
    )

    def tangents(i):
        at, tan_at = pl.ds(pl.multiple_of(i * block, 8), half), pl.ds(pl.multiple_of(i * block + half, 8), half)
        gate_pre, gate_tan = s.gate[at, :], s.gate[tan_at, :]
        up_pre, up_tan = s.up[at, :], s.up[tan_at, :]
        dh, dh_tan = s.grad[at, :], s.grad[tan_at, :]
        silu_val, silu_one, silu_two = silu_terms(gate_pre)
        da_tan = (dh_tan * up_pre + dh * up_tan) * silu_one + dh * up_pre * silu_two * gate_tan
        db_tan = dh_tan * silu_val + dh * silu_one * gate_tan
        to = pl.ds(pl.multiple_of(i * half, 8), half)
        s.da_tan[to, :] = da_tan
        s.db_tan[to, :] = db_tan

    each(0, nyc, tangents)

    def b_part(k, q):
        da_tan, db_tan = s.da_tan[...].astype(BF), s.db_tan[...].astype(BF)
        sides = []
        for h in range(2):
            features = pl.ds(pl.multiple_of(q * quarter + h * (quarter // 2) + k * bw, 128), bw)
            term = dot_last(da_tan, s.w_gate[features, :]) + dot_last(db_tan, s.w_up[features, :])
            sides.append(term.reshape(nyc, half, bw))
        s.part_b[k, pl.ds(q, 1)] = jnp.concatenate(sides, 1).astype(BF).reshape(1, rows, bw)

    def b_start(k):
        b_part(k, ring.opp)
        scat_b.start(k, 0)
        scat_b.start(k, 1)
        b_part(k, ring.left)
        scat_b.start(k, 2)
        b_part(k, ring.right)
        scat_b.start(k, 3)
        b_part(k, ring.me)

    def return_b(k):
        s.bak_a[k] = scat_b.finish(k).astype(BF).reshape(nyc, block, bw)
        bak_yc.start(k)

    def pass_b(k):
        bak_yc.wait(k)
        swap(s.bak_b, s.bak_c, k, bw)
        bak_z.start(k)

    def grad_in(k):
        bak_z.wait(k)
        both = combine(s.bak_d[k].reshape(rows, bw))
        for h in range(2):
            columns = pl.ds(h * (quarter // 2) + k * bw, bw)
            s.dx[:, columns] = (s.y_tan[:, columns] + both[h * tokens : (h + 1) * tokens]).astype(BF)

    pipeline((b_start, scat_b.middle, return_b, pass_b, grad_in), back_chunks)
    gather_a.finish(0)

    per = quarter // (nz * nyc)
    run = nz * per

    def products(c):
        for m in range(N_MP):
            columns = pl.ds(pl.multiple_of(c * (quarter // N_CORE), 128), quarter // N_CORE)
            value = dot_first(s.attn_full[0, m, :, columns], s.dx[...]).astype(BF)
            s.prod[pl.ds(c, 1), :, pl.ds(m * run, run), :] = value.reshape(1, ny, run, quarter)

    other = 1 - core

    def core_copy():
        return pltpu.make_async_remote_copy(
            src_ref=s.prod.at[other],
            dst_ref=s.core_in,
            send_sem=s.core_ssem,
            recv_sem=s.core_rsem,
            device_id=at_yc(y * N_CORE + other),
            device_id_type=MESH,
        )

    products(other)
    core_copy().start()
    products(core)
    core_copy().wait_recv()

    def add_core(i):
        value = s.prod[pl.ds(core, 1), pl.ds(i, 1)].astype(F32)[0] + s.core_in[pl.ds(i, 1)].astype(F32)
        s.sum_y[0, pl.ds(i, 1)] = value.astype(BF)

    each(0, ny, add_core)
    ex_y = Exchange(s.sum_y, s.in_y, sems("ex_y"), ny, y, lambda to: at_yc(to * N_CORE + core))
    ex_z = Exchange(s.sum_z, s.in_z, sems("ex_z"), nz, z, at_z)
    ex_y.start(0)
    ex_y.wait(0)
    total = jnp.sum(s.in_y[0].astype(F32), axis=0)
    total = total.reshape(N_MP, nz, per, quarter)
    total = jnp.stack([total[m] for m in range(N_MP)], 1)
    s.sum_z[0] = total.reshape(nz, N_MP * per, quarter).astype(BF)
    ex_z.start(0)
    ex_z.wait(0)
    total = jnp.sum(s.in_z[0].astype(F32), axis=0)
    s.last_a[0] = (total * (1.0 / math.sqrt(tokens * nz * nyc))).reshape(N_MP, per, quarter)
    last = Exchange(s.last_a, s.last_b, sems("last"), N_MP, me_m, lambda to: (me_e, to))
    last.start(0)
    last.wait(0)
    for m in range(N_MP):
        out[0, :, m * quarter : (m + 1) * quarter] = s.last_b[0, m]

    for k in range(chunks):
        for stage in (scat_z, go_z, go_yc, gather_x, scat_o, ret_yc, ret_z, cot_z, cot_yc, gather_c):
            stage.drain(k)
    for k in range(back_chunks):
        for stage in (scat_b, bak_yc, bak_z):
            stage.drain(k)
    gather_a.drain(0)
    core_copy().wait_send()
    ex_y.drain(0)
    ex_z.drain(0)
    last.drain(0)


def scratch(sizes):
    nz, nyc, cap, tokens, quarter, hidden, chunks, back_chunks = sizes
    ny = nyc // N_CORE
    cw, bw = quarter // chunks, quarter // 2 // back_chunks
    block = 2 * nz * cap
    rows = nyc * block
    model = N_MP * quarter
    per = quarter // (nz * nyc)
    names = Names()

    def vmem(name, shape, kind=BF):
        names.add(name, pltpu.VMEM(shape, kind))

    def sems(name, k, n):
        names.add(name + "_ssem", pltpu.SemaphoreType.DMA((k, n)))
        names.add(name + "_rsem", pltpu.SemaphoreType.DMA((k, n)))

    names.add("load_sem", pltpu.SemaphoreType.DMA((6,)))
    vmem("attn", (tokens, quarter))
    vmem("out_proj", (quarter, model))
    vmem("tan_proj", (quarter, model))
    vmem("w_gate", (model, hidden))
    vmem("w_up", (model, hidden))
    vmem("w_down", (hidden, model))
    vmem("swap", (rows, rows))
    for tag, count, height, width in (
        ("z", chunks, 2 * tokens, cw),
        ("o", chunks, rows, cw),
        ("b", back_chunks, rows, bw),
    ):
        vmem("part_" + tag, (count, N_MP, height, width))
        vmem("hop_" + tag, (count, 2, height // 2, width))
        vmem("total_" + tag, (count, 2, height, width))
        sems("scat_" + tag, count, 6)
    for tag, count, width in (("go", chunks, cw), ("ret", chunks, cw), ("cot", chunks, cw), ("bak", back_chunks, bw)):
        for letter in "abcd":
            vmem(f"{tag}_{letter}", (count, nz, block, width))
        sems(tag + "_z", count, nz)
        sems(tag + "_yc", count, nyc)
    for tag in "xc":
        vmem(tag + "_full", (chunks, N_MP, rows, cw))
        sems("gather_" + tag, chunks, 6)
    vmem("attn_full", (1, N_MP, tokens, quarter))
    sems("gather_a", 1, 6)
    vmem("x_in", (chunks, 2 * tokens, cw))
    vmem("gate", (rows, hidden), F32)
    vmem("up", (rows, hidden), F32)
    vmem("grad", (rows, hidden), F32)
    vmem("hidden", (rows, hidden))
    vmem("da_tan", (rows // 2, hidden), F32)
    vmem("db_tan", (rows // 2, hidden), F32)
    vmem("y_tan", (tokens, quarter), F32)
    vmem("dx", (tokens, quarter))
    run = N_MP * nz * per
    vmem("prod", (N_CORE, ny, run, quarter))
    vmem("core_in", (ny, run, quarter))
    names.add("core_ssem", pltpu.SemaphoreType.DMA)
    names.add("core_rsem", pltpu.SemaphoreType.DMA)
    vmem("sum_y", (1, ny, run, quarter))
    vmem("in_y", (1, ny, run, quarter))
    sems("ex_y", 1, ny)
    vmem("sum_z", (1, nz, N_MP * per, quarter))
    vmem("in_z", (1, nz, N_MP * per, quarter))
    sems("ex_z", 1, nz)
    vmem("last_a", (1, N_MP, per, quarter), F32)
    vmem("last_b", (1, N_MP, per, quarter), F32)
    sems("last", 1, N_MP)
    return names


def local(nz, nyc, attn, out_proj, tangent_proj, resid, target, routes, gates, w_gate, w_up, w_down):
    tokens, quarter = attn.shape
    hidden = w_gate.shape[2]
    experts = nz * nyc
    cap = max(2, 5 * 2 * tokens // (4 * experts))
    half = nyc * cap
    rows = nz * 2 * half
    sizes = (nz, nyc, cap, tokens, quarter, hidden, CHUNKS, BACK_CHUNKS)

    flat = routes.reshape(-1)
    number = jnp.arange(flat.shape[0])
    earlier = (flat[:, None] == flat[None, :]) & (number[None, :] < number[:, None])
    slot = flat * cap + jnp.sum(earlier.astype(jnp.int32), axis=1)
    place = (slot // half) * (2 * half) + slot % half
    place = place.reshape(tokens, 2)
    place = jnp.stack([place, place + half], 0).reshape(2 * tokens, 2)
    line = jnp.arange(rows)
    back0 = (place[:, 0:1] == line[None, :]).astype(BF)
    back1 = (place[:, 1:2] == line[None, :]).astype(BF)
    pick = ((line[:, None] == place[None, :, 0]) | (line[:, None] == place[None, :, 1])).astype(BF)
    gates2 = jnp.concatenate([gates, gates], 0)
    slot_gate = jnp.sum(
        jnp.where(line[:, None] == place[None, :, 0], gates2[None, :, 0], 0.0)
        + jnp.where(line[:, None] == place[None, :, 1], gates2[None, :, 1], 0.0),
        axis=1,
        keepdims=True,
    )
    names = scratch(sizes)
    vmem, anywhere = pl.BlockSpec(memory_space=pltpu.VMEM), pl.BlockSpec(memory_space=pl.ANY)
    return pl.pallas_call(
        functools.partial(kernel, sizes, names),
        out_shape=jax.ShapeDtypeStruct((1, quarter // experts, N_MP * quarter), F32),
        in_specs=[anywhere] * 3 + [vmem] * 7 + [anywhere] * 3,
        out_specs=vmem,
        scratch_shapes=names.shapes,
        compiler_params=pltpu.CompilerParams(
            collective_id=0, has_side_effects=True, vmem_limit_bytes=60 * 2**20
        ),
        cost_estimate=pl.CostEstimate(flops=6_000_000_000, bytes_accessed=12_000_000, transcendentals=300_000),
    )(
        attn, out_proj, tangent_proj, resid, target, pick, back0, back1, slot_gate, gates2, w_gate, w_up, w_down
    )


def solution(mesh):
    experts = mesh.shape["expert"]
    nz = 1 << ((experts.bit_length() - 1) // 2)
    in_specs = (
        P("expert", "mp"),
        P("mp", None),
        P("mp", None),
        P("expert", "mp"),
        P("expert", "mp"),
        P("expert", None),
        P("expert", None),
        P("expert", None, "mp"),
        P("expert", None, "mp"),
        P("expert", "mp", None),
    )
    return jax.shard_map(
        functools.partial(local, nz, experts // nz),
        mesh=mesh,
        in_specs=in_specs,
        out_specs=P("mp", "expert", None),
        check_vma=False,
    )
```

time: 736 us -> 217 us (0.29)
  waiting for transfers between devices: 375 us -> 0 us
  blocking collectives: 208 us -> 0 us
  Pallas kernels: 0 us -> 205 us
  local copies, waits for them, and re-layouts: 55.1 us -> 8.91 us
  starting transfers between devices: 37.9 us -> 0 us
  matrix products: 29.1 us -> 0 us
  between operations: 14.7 us -> 0.04 us
  other arithmetic: 14.2 us -> 3.02 us
    pallas_call x0 -> x1, Pallas kernels: none -> 205 us  [local(): pl.pallas_call(functools.partial(kernel, sizes, names), out_shape=jax.Sha...]
    unnamed x7 -> x0, waiting for transfers between devices: 191 us -> none
    all_to_all x3 -> x0, blocking collectives: 156 us -> none  [the longest x1 63.7 us: local(): lax.all_to_all(spread(x_full), 'expert', split_axis=0, concat_axis=0, til...]
    all_to_all x4 -> x0, waiting for transfers between devices: 98.1 us -> none  [the longest x1 42.6 us: local(): lax.all_to_all(weighted(y_tan_full), 'expert', split_axis=0, concat_axis=...]
    reduce_scatter x5 -> x0, waiting for transfers between devices: 86.6 us -> none  [the longest x1 21.9 us: local(): lax.psum_scatter(back_part.astype(jnp.bfloat16), 'mp', scatter_dimension=...]
    all_gather x5 -> x0, blocking collectives: 52.2 us -> none  [the longest x1 11.3 us: local(): lax.all_gather(x_tan_part, 'mp', axis=1, tiled=True)]
    all_to_all x4 -> x0, starting transfers between devices: 37.5 us -> none  [the longest x1 12.1 us: local(): lax.all_to_all(out_tan, 'expert', split_axis=0, concat_axis=0, tiled=True)]
    dot_general x13 -> x0, matrix products: 29.1 us -> none  [the longest x4 9.36 us: contract_last(): lax.dot_general(left, right, (((1,), (1,)), ((), ())), preferred_element_...]
  transfers between devices with their start and end apart: 10 -> 0, of which waited for: 10 -> 0; matrix products, arithmetic and copies ran while one was open for 5% -> 0% of each run, Pallas kernels for 0% -> 0%
where the time goes in v1:
time: 217 us
  Pallas kernels  205 us (94%)
  local copies, waits for them, and re-layouts  8.91 us (4%)
  other arithmetic  3.02 us (1%)
    pallas_call x1, Pallas kernels, local(): pl.pallas_call(functools.partial(kernel, sizes, names), out_shape=jax.Sha...  205 us
    unnamed x9, local copies, waits for them, and re-layouts  6.2 us

profile of v1, /device:TPU:1, one launch (start us, length us, event | category | flops | bytes accessed | tf_op | source)
XLA Modules:
  0.0 216.9 jit_solution(14344664330221220184)
XLA Ops:
  0.0 0.0 copy-start
  0.0 0.8 constant_dynamic-update-slice_fusion.1
  0.8 0.7 constant_dynamic-update-slice_fusion
  1.5 0.8 copy.42
  2.3 0.1 eq.39
  2.4 0.2 convert_reduce_fusion
  2.6 0.1 reduce_sum.21
  2.7 0.1 copy.43
  2.8 0.7 add_bitcast_fusion.1
  3.6 0.2 add_reduce_fusion
  3.8 0.8 copy.45.refs_9_
  4.6 0.9 broadcast_in_dim.39.refs_8_
  5.4 0.9 fusion.1.refs_5_
  6.3 1.0 fusion.2
  7.3 0.0 copy-start.1
  7.3 0.0 copy-done
  7.3 1.6 copy.46.refs_10_
  8.9 0.0 copy-done.1
  8.9 1.6 copy.47.refs_11_
  10.5 205.0 %shard_map.100 = f32[1,8,2048]{2,1,0:T(8,128)} custom-call(bf16[128,512]{1,0:T(8,128)(2,1)} %refs_0_.1, bf16[512,2048]{1,0:T(8,128)(2,1)} %refs_1_.1, bf16[512,2048]{1,0:T(8,128)(2,1)} %refs_2_.1, bf16[128,512]{1,0:T(8,128)(2,1)} %refs_3_.1, bf16[128,512]{1,0:T(8,128)(2,1)} %refs_4_.1, bf16[640,256]{1,0:T(8,128)(2,1)} %fusion.1.refs_5_, ...), custom_call_target="tpu_custom_call" | custom-call | flops 6000000000 | bytes 12000000 | tf_op jit(solution)/shard_map/pallas_call | solution.py:702
  215.5 1.5 copy.50
  (3 shorter events, 0.0 us)
Async XLA Ops:
  0.0 7.3 %copy-start = (bf16[1,2048,352]{1,2,0:T(8,128)(2,1)S(1)}, bf16[1,2048,352]{1,2,0:T(8,128)(2,1)}, u32[]{:S(2)}) copy-start(bf16[1,2048,352]{1,2,0:T(8,128)(2,1)} %param.17) | copy-start | bytes 4325380
  7.3 1.6 copy-start.1

commit v2 on v1

--- a/solution.py
+++ b/solution.py
@@ -13,8 +13,11 @@
 F32 = jnp.float32
 N_MP = 4
 N_CORE = 2
-CHUNKS = 2
+CHUNKS = 4
 BACK_CHUNKS = 2
+ORDER_IN = (2, 3, 2, 1, 0, 2, 0, 1, 1, 2, 3, 1, 0, 3, 2, 3, 0, 1, 2, 1, 3, 2, 0, 1, 3, 0, 3, 1, 2, 0, 3, 0)
+ORDER_OUT = (0, 3, 0, 0, 3, 3, 0, 2, 2, 3, 1, 0, 2, 3, 1, 1, 2, 0, 3, 1, 2, 1, 0, 3, 2, 3, 0, 1, 2, 3, 0, 1, 2, 1, 2, 1, 3, 0, 2, 1)
+ORDER_BACK = (0, 0, 1, 0, 1, 1, 0, 1, 0, 1, 0, 1, 0, 0, 1, 1, 0, 1)
 
 
 class Names:
@@ -58,11 +61,11 @@
     lax.fori_loop(lower, upper, step, 0)
 
 
-def pipeline(stages, chunks):
-    for turn in range(len(stages) + chunks - 1):
-        for k in range(chunks):
-            if 0 <= turn - k < len(stages):
-                stages[turn - k](k)
+def pipeline(stages, order):
+    done = [0] * (max(order) + 1)
+    for k in order:
+        stages[done[k]](k)
+        done[k] += 1
 
 
 class Exchange:
@@ -97,6 +100,30 @@
 
     def drain(self, k):
         each(1, self.n, lambda d: self.out(k, d).wait_send())
+
+
+class SpreadY(Exchange):
+    def __init__(self, ref, core, sems, n, me, device):
+        super().__init__(ref, ref, sems, n, me, device)
+        self.core = core
+
+    def copy(self, k, d, block, landing, device):
+        ref = self.src.at[k, self.core, block]
+        return pltpu.make_async_remote_copy(
+            src_ref=ref,
+            dst_ref=ref,
+            send_sem=self.ssem.at[k, d],
+            recv_sem=self.rsem.at[k, d],
+            device_id=device,
+            device_id_type=MESH,
+        )
+
+    def out(self, k, d):
+        to = lax.rem(self.me + d, self.n)
+        return self.copy(k, d, self.me, self.me, self.device(to))
+
+    def start(self, k):
+        each(1, self.n, lambda d: self.out(k, d).start())
 
 
 class Ring:
@@ -225,10 +252,9 @@
 
 
 def kernel(sizes, names, *refs):
-    (attn_h, out_proj_h, tan_proj_h, resid, target, pick, back0, back1, slot_gate, gates) = refs[:10]
-    w_gate_h, w_up_h, w_down_h, out = refs[10:14]
+    attn_h, out_proj_h, tan_proj_h, resid, target, routes, gates, w_gate_h, w_up_h, w_down_h, out = refs[:11]
     s = names
-    s.bind(refs[14:])
+    s.bind(refs[11:])
     nz, nyc, cap, tokens, quarter, hidden, chunks, back_chunks = sizes
     ny = nyc // N_CORE
     cw = quarter // chunks
@@ -266,6 +292,11 @@
         load.start()
 
     barrier = pltpu.get_barrier_semaphore()
+    counts = {}
+
+    def nth(stage):
+        counts[stage] = counts.get(stage, -1) + 1
+        return counts[stage]
 
     def greet(device):
         pl.semaphore_signal(barrier, inc=1, device_id=device, device_id_type=MESH)
@@ -273,7 +304,6 @@
     each(1, nz, lambda d: greet(at_z(lax.rem(z + d, nz))))
     each(1, nyc, lambda d: greet(at_yc(lax.rem(yc + d, nyc))))
     each(1, N_MP, lambda d: greet((me_e, lax.rem(me_m + d, N_MP))))
-    pl.semaphore_wait(barrier, nz + nyc + N_MP - 3)
 
     def sems(name):
         return getattr(s, name + "_ssem"), getattr(s, name + "_rsem")
@@ -291,7 +321,11 @@
     scat_b = Scatter(ring, s.part_b, s.hop_b, s.total_b, sems("scat_b"), rows)
     bak_yc = Exchange(s.bak_a, s.bak_b, sems("bak_yc"), nyc, yc, at_yc)
     bak_z = Exchange(s.bak_c, s.bak_d, sems("bak_z"), nz, z, at_z)
-    gather_a = Gather(ring, s.attn_full, sems("gather_a"), tokens)
+    att_yc = Exchange(s.att_a, s.att_b, sems("att_yc"), nyc, yc, at_yc)
+    gather_a = Gather(ring, s.att_full, sems("gather_a"), quarter)
+    spread_y = SpreadY(s.dx, core, sems("spread_y"), ny, y, lambda to: at_yc(to * N_CORE + core))
+    ex_z = Exchange(s.sum_z, s.in_z, sems("ex_z"), nz, z, at_z)
+    last = Exchange(s.last_a, s.last_b, sems("last"), N_MP, me_m, lambda to: (me_e, to))
 
     def swap(src, dst, k, width):
         value = dot(s.swap[...], src[k].reshape(rows, width))
@@ -306,29 +340,97 @@
         s.part_z[k, pl.ds(q, 1), pl.ds(0, tokens), :] = dot(s.attn[...], s.out_proj[:, columns]).astype(BF)[None]
         s.part_z[k, pl.ds(q, 1), pl.ds(tokens, tokens), :] = dot(s.attn[...], s.tan_proj[:, columns]).astype(BF)[None]
 
-    def z_start(k):
+    def z_first(k):
         z_part(k, ring.opp)
+        if nth("z_first") == 0:
+            pl.semaphore_wait(barrier, nz + nyc + N_MP - 3)
         scat_z.start(k, 0)
         scat_z.start(k, 1)
+
+    def z_second(k):
         z_part(k, ring.left)
         scat_z.start(k, 2)
         z_part(k, ring.right)
         scat_z.start(k, 3)
         z_part(k, ring.me)
+        if nth("z_second") == 0:
+            route_rows()
+
+    def route_rows():
+        eye = iota((tokens, tokens), 0) == iota((tokens, tokens), 1)
+        earlier_row = (iota((tokens, tokens), 1) < iota((tokens, tokens), 0)).astype(F32)
+        earlier_column = (iota((tokens, tokens), 0) < iota((tokens, tokens), 1)).astype(F32)
+
+        def column(row, zero):
+            return jnp.sum(jnp.where(eye, row, zero), axis=1, keepdims=True)
+
+        first, second = routes[0:1, :], routes[1:2, :]
+        gate_rows = gates[0:1, :], gates[1:2, :]
+        names_f = [first.astype(F32), second.astype(F32)]
+        columns_f = [column(row, 0.0) for row in names_f]
+        same = [[(columns_f[i] == names_f[j]).astype(F32) for j in range(2)] for i in range(2)]
+
+        def line_of(name, position):
+            wide, narrow = lax.div(name, nyc), lax.rem(name, nyc)
+            return wide * block + narrow * cap + position
+
+        place_row = [
+            line_of(first, jnp.sum(same[0][0] * earlier_column, axis=0, keepdims=True).astype(jnp.int32)),
+            line_of(
+                second,
+                (
+                    jnp.sum(same[0][1], axis=0, keepdims=True)
+                    + jnp.sum(same[1][1] * earlier_column, axis=0, keepdims=True)
+                ).astype(jnp.int32),
+            ),
+        ]
+        place_column = [
+            line_of(
+                columns_f[0].astype(jnp.int32),
+                jnp.sum(same[0][0] * earlier_row, axis=1, keepdims=True).astype(jnp.int32),
+            ),
+            line_of(
+                columns_f[1].astype(jnp.int32),
+                (
+                    jnp.sum(same[1][0], axis=1, keepdims=True)
+                    + jnp.sum(same[1][1] * earlier_row, axis=1, keepdims=True)
+                ).astype(jnp.int32),
+            ),
+        ]
+        across, down = iota((tokens, rows), 1), iota((rows, tokens), 0)
+        weight = jnp.zeros((rows, 1), F32)
+        for h in range(2):
+            at = pl.ds(h * tokens, tokens)
+            s.back0[at, :] = (across == place_column[0] + h * half).astype(F32).astype(BF)
+            s.back1[at, :] = (across == place_column[1] + h * half).astype(F32).astype(BF)
+            hits = [down == place_row[i] + h * half for i in range(2)]
+            s.pick[:, at] = (hits[0] | hits[1]).astype(F32).astype(BF)
+            chosen = jnp.where(hits[0], gate_rows[0], 0.0) + jnp.where(hits[1], gate_rows[1], 0.0)
+            weight = weight + jnp.sum(chosen, axis=1, keepdims=True)
+        s.slot_gate[...] = weight
+        both = [column(row, 0.0) for row in gate_rows]
+        for i in range(2):
+            s.gate_column[i] = jnp.concatenate([both[i], both[i]], 0)
+
+    def swap_rows():
+        r = iota((rows, 1), 0)
+        a, h, b, p = r // block, (r % block) // half, (r % half) // cap, r % cap
+        s.swap[...] = (iota((rows, rows), 1) == b * block + h * half + a * cap + p).astype(F32).astype(BF)
 
     def spread_x(k):
-        if k == 0:
-            r = iota((rows, 1), 0)
-            a, h, b, p = r // block, (r % block) // half, (r % half) // cap, r % cap
-            s.swap[...] = (iota((rows, rows), 1) == b * block + h * half + a * cap + p).astype(F32).astype(BF)
         value = scat_z.finish(k)
         columns = pl.ds(k * cw, cw)
         s.x_in[k, pl.ds(0, tokens), :] = (
             resid[:, columns].astype(F32) + value[:tokens]
         ).astype(BF)
         s.x_in[k, pl.ds(tokens, tokens), :] = value[tokens:].astype(BF)
-        s.go_a[k] = dot(pick[...], s.x_in[k]).astype(BF).reshape(nz, block, cw)
+        s.go_a[k] = dot(s.pick[...], s.x_in[k]).astype(BF).reshape(nz, block, cw)
         go_z.start(k)
+        before = nth("spread_x")
+        if before == 0:
+            swap_rows()
+        if before == chunks - 1:
+            attn_send()
 
     def pass_x(k):
         go_z.wait(k)
@@ -344,7 +446,8 @@
 
     def pre_acts(k):
         gather_x.finish(k)
-        if k == 0:
+        before = nth("pre_acts")
+        if before == 0:
             loads[3].wait()
             loads[4].wait()
 
@@ -355,9 +458,9 @@
             for m in range(N_MP):
                 features = pl.ds(m * quarter + k * cw, cw)
                 values = s.x_full[k, m, at, :]
-                gate = gate + dot(values, s.w_gate[features, :])
-                up = up + dot(values, s.w_up[features, :])
-            if k:
+                gate = gate + dot_last(values, s.w_gate[:, features])
+                up = up + dot_last(values, s.w_up[:, features])
+            if before:
                 gate = gate + s.gate[at, :]
                 up = up + s.up[at, :]
             s.gate[at, :] = gate
@@ -365,38 +468,24 @@
 
         each(0, rows // step_rows, body)
 
-    def permute_attn():
-        r = iota((1, quarter), 1)
-        per = quarter // (nz * nyc)
-        c, yy, zz, p = (
-            r // (quarter // N_CORE),
-            (r // (nz * per)) % ny,
-            (r // per) % nz,
-            r % per,
-        )
-        wanted = ((zz * ny + yy) * N_CORE + c) * per + p
-        permute = (iota((quarter, quarter), 0) == wanted).astype(F32).astype(BF)
-        s.attn_full[0, pl.ds(me_m, 1)] = dot(s.attn[...], permute).astype(BF)[None]
-
-    def attn_start(k):
-        if k == chunks - 1:
-            permute_attn()
-            gather_a.start(0)
-
-    pipeline(
-        (
-            z_start,
-            scat_z.middle,
-            spread_x,
-            attn_start,
-            pass_x,
-            gather_start_x,
-            gather_x.middle,
-            pre_acts,
-        ),
-        chunks,
-    )
-    gather_a.middle(0)
+    per = quarter // (nz * nyc)
+    run = nz * per
+
+    def attn_send():
+        r = iota((quarter, 1), 0)
+        c, zz, p = r // run, (r % run) // per, r % per
+        wanted = (zz * nyc + c) * per + p
+        permute = (iota((quarter, quarter), 1) == wanted).astype(F32).astype(BF)
+        s.att_a[0] = dot_last(permute, s.attn[...]).astype(BF).reshape(nyc, run, tokens)
+        att_yc.start(0)
+
+    def attn_gather():
+        att_yc.wait(0)
+        s.att_full[0, pl.ds(me_m, 1)] = s.att_b[0].reshape(1, nyc * run, tokens)
+        gather_a.start(0)
+
+    pipeline((z_first, z_second, scat_z.middle, spread_x, pass_x, gather_start_x, gather_x.middle, pre_acts), ORDER_IN)
+    attn_gather()
 
     def activations(i):
         at, tan_at = pl.ds(pl.multiple_of(i * block, 8), half), pl.ds(pl.multiple_of(i * block + half, 8), half)
@@ -414,10 +503,12 @@
         columns = pl.ds(pl.multiple_of(q * quarter + k * cw, 128), cw)
         s.part_o[k, pl.ds(q, 1)] = dot(s.hidden[...], s.w_down[:, columns]).astype(BF)[None]
 
-    def o_start(k):
+    def o_first(k):
         o_part(k, ring.opp)
         scat_o.start(k, 0)
         scat_o.start(k, 1)
+
+    def o_second(k):
         o_part(k, ring.left)
         scat_o.start(k, 2)
         o_part(k, ring.right)
@@ -434,7 +525,7 @@
         ret_z.start(k)
 
     def combine(values):
-        return gates[:, 0:1] * dot(back0[...], values) + gates[:, 1:2] * dot(back1[...], values)
+        return s.gate_column[0] * dot(s.back0[...], values) + s.gate_column[1] * dot(s.back1[...], values)
 
     def residual(k):
         ret_z.wait(k)
@@ -443,7 +534,7 @@
         s.y_tan[:, columns] = both[tokens:]
         diff = both[:tokens] - target[:, columns].astype(F32)
         sent = jnp.concatenate([diff, both[tokens:]], 0).astype(BF)
-        s.cot_a[k] = (dot(pick[...], sent) * slot_gate[...]).astype(BF).reshape(nz, block, cw)
+        s.cot_a[k] = (dot(s.pick[...], sent) * s.slot_gate[...]).astype(BF).reshape(nz, block, cw)
         cot_z.start(k)
 
     def pass_c(k):
@@ -458,6 +549,7 @@
 
     def grad_hidden(k):
         gather_c.finish(k)
+        before = nth("grad_hidden")
 
         def body(i):
             at = pl.ds(pl.multiple_of(i * step_rows, step_rows), step_rows)
@@ -465,7 +557,7 @@
             for m in range(N_MP):
                 features = pl.ds(m * quarter + k * cw, cw)
                 grad = grad + dot_last(s.c_full[k, m, at, :], s.w_down[:, features])
-            if k:
+            if before:
                 grad = grad + s.grad[at, :]
             s.grad[at, :] = grad
 
@@ -473,7 +565,8 @@
 
     pipeline(
         (
-            o_start,
+            o_first,
+            o_second,
             scat_o.middle,
             return_o,
             pass_o,
@@ -483,8 +576,9 @@
             gather_c.middle,
             grad_hidden,
         ),
-        chunks,
+        ORDER_OUT,
     )
+    gather_a.middle(0)
 
     def tangents(i):
         at, tan_at = pl.ds(pl.multiple_of(i * block, 8), half), pl.ds(pl.multiple_of(i * block + half, 8), half)
@@ -505,14 +599,16 @@
         sides = []
         for h in range(2):
             features = pl.ds(pl.multiple_of(q * quarter + h * (quarter // 2) + k * bw, 128), bw)
-            term = dot_last(da_tan, s.w_gate[features, :]) + dot_last(db_tan, s.w_up[features, :])
+            term = dot(da_tan, s.w_gate[:, features]) + dot(db_tan, s.w_up[:, features])
             sides.append(term.reshape(nyc, half, bw))
         s.part_b[k, pl.ds(q, 1)] = jnp.concatenate(sides, 1).astype(BF).reshape(1, rows, bw)
 
-    def b_start(k):
+    def b_first(k):
         b_part(k, ring.opp)
         scat_b.start(k, 0)
         scat_b.start(k, 1)
+
+    def b_second(k):
         b_part(k, ring.left)
         scat_b.start(k, 2)
         b_part(k, ring.right)
@@ -533,55 +629,57 @@
         both = combine(s.bak_d[k].reshape(rows, bw))
         for h in range(2):
             columns = pl.ds(h * (quarter // 2) + k * bw, bw)
-            s.dx[:, columns] = (s.y_tan[:, columns] + both[h * tokens : (h + 1) * tokens]).astype(BF)
-
-    pipeline((b_start, scat_b.middle, return_b, pass_b, grad_in), back_chunks)
-    gather_a.finish(0)
-
-    per = quarter // (nz * nyc)
-    run = nz * per
-
-    def products(c):
-        for m in range(N_MP):
-            columns = pl.ds(pl.multiple_of(c * (quarter // N_CORE), 128), quarter // N_CORE)
-            value = dot_first(s.attn_full[0, m, :, columns], s.dx[...]).astype(BF)
-            s.prod[pl.ds(c, 1), :, pl.ds(m * run, run), :] = value.reshape(1, ny, run, quarter)
+            value = (s.y_tan[:, columns] + both[h * tokens : (h + 1) * tokens]).astype(BF)
+            s.dx[k, pl.ds(core, 1), pl.ds(y, 1), :, pl.ds(h * bw, bw)] = value.reshape(1, 1, tokens, bw)
+        spread_y.start(k)
 
     other = 1 - core
 
-    def core_copy():
+    def core_copy(k, side):
         return pltpu.make_async_remote_copy(
-            src_ref=s.prod.at[other],
-            dst_ref=s.core_in,
-            send_sem=s.core_ssem,
-            recv_sem=s.core_rsem,
+            src_ref=s.dx.at[k, side],
+            dst_ref=s.dx.at[k, side],
+            send_sem=s.core_ssem.at[k],
+            recv_sem=s.core_rsem.at[k],
             device_id=at_yc(y * N_CORE + other),
             device_id_type=MESH,
         )
 
-    products(other)
-    core_copy().start()
-    products(core)
-    core_copy().wait_recv()
-
-    def add_core(i):
-        value = s.prod[pl.ds(core, 1), pl.ds(i, 1)].astype(F32)[0] + s.core_in[pl.ds(i, 1)].astype(F32)
-        s.sum_y[0, pl.ds(i, 1)] = value.astype(BF)
-
-    each(0, ny, add_core)
-    ex_y = Exchange(s.sum_y, s.in_y, sems("ex_y"), ny, y, lambda to: at_yc(to * N_CORE + core))
-    ex_z = Exchange(s.sum_z, s.in_z, sems("ex_z"), nz, z, at_z)
-    ex_y.start(0)
-    ex_y.wait(0)
-    total = jnp.sum(s.in_y[0].astype(F32), axis=0)
-    total = total.reshape(N_MP, nz, per, quarter)
-    total = jnp.stack([total[m] for m in range(N_MP)], 1)
-    s.sum_z[0] = total.reshape(nz, N_MP * per, quarter).astype(BF)
-    ex_z.start(0)
-    ex_z.wait(0)
-    total = jnp.sum(s.in_z[0].astype(F32), axis=0)
-    s.last_a[0] = (total * (1.0 / math.sqrt(tokens * nz * nyc))).reshape(N_MP, per, quarter)
-    last = Exchange(s.last_a, s.last_b, sems("last"), N_MP, me_m, lambda to: (me_e, to))
+    def dx_core(k):
+        spread_y.wait(k)
+        core_copy(k, core).start()
+
+    def attn_rows():
+        gather_a.finish(0)
+        for c in range(N_CORE):
+            for yy in range(ny):
+                columns = pl.ds((c * ny + yy) * tokens, tokens)
+                for m in range(N_MP):
+                    source = pl.ds((yy * N_CORE + c) * run, run)
+                    s.att_rows[pl.ds(m * run, run), columns] = s.att_full[0, m, source, :]
+
+    def product(k):
+        if nth("product") == 0:
+            attn_rows()
+        core_copy(k, other).wait_recv()
+        value = dot(s.att_rows[...], s.dx[k].reshape(nyc * tokens, 2 * bw))
+        value = value.reshape(N_MP, nz, per, 2 * bw)
+        value = jnp.stack([value[m] for m in range(N_MP)], 1)
+        s.sum_z[k] = value.reshape(nz, N_MP * per, 2 * bw).astype(BF)
+        ex_z.start(k)
+
+    def total_z(k):
+        ex_z.wait(k)
+        total = jnp.sum(s.in_z[k].astype(F32), axis=0) * (1.0 / math.sqrt(tokens * nz * nyc))
+        total = total.reshape(N_MP, per, 2 * bw)
+        for h in range(2):
+            columns = pl.ds(h * (quarter // 2) + k * bw, bw)
+            s.last_a[0, :, :, columns] = total[:, :, h * bw : (h + 1) * bw]
+
+    pipeline(
+        (b_first, b_second, scat_b.middle, return_b, pass_b, grad_in, dx_core, product, total_z),
+        ORDER_BACK,
+    )
     last.start(0)
     last.wait(0)
     for m in range(N_MP):
@@ -591,12 +689,11 @@
         for stage in (scat_z, go_z, go_yc, gather_x, scat_o, ret_yc, ret_z, cot_z, cot_yc, gather_c):
             stage.drain(k)
     for k in range(back_chunks):
-        for stage in (scat_b, bak_yc, bak_z):
+        for stage in (scat_b, bak_yc, bak_z, spread_y, ex_z):
             stage.drain(k)
+        core_copy(k, core).wait_send()
+    att_yc.drain(0)
     gather_a.drain(0)
-    core_copy().wait_send()
-    ex_y.drain(0)
-    ex_z.drain(0)
     last.drain(0)
 
 
@@ -621,8 +718,8 @@
     vmem("attn", (tokens, quarter))
     vmem("out_proj", (quarter, model))
     vmem("tan_proj", (quarter, model))
-    vmem("w_gate", (model, hidden))
-    vmem("w_up", (model, hidden))
+    vmem("w_gate", (hidden, model))
+    vmem("w_up", (hidden, model))
     vmem("w_down", (hidden, model))
     vmem("swap", (rows, rows))
     for tag, count, height, width in (
@@ -642,8 +739,18 @@
     for tag in "xc":
         vmem(tag + "_full", (chunks, N_MP, rows, cw))
         sems("gather_" + tag, chunks, 6)
-    vmem("attn_full", (1, N_MP, tokens, quarter))
+    run = nz * per
+    for letter in "ab":
+        vmem("att_" + letter, (1, nyc, run, tokens))
+    sems("att_yc", 1, nyc)
+    vmem("att_full", (1, N_MP, nyc * run, tokens))
     sems("gather_a", 1, 6)
+    vmem("att_rows", (N_MP * run, nyc * tokens))
+    vmem("pick", (rows, 2 * tokens))
+    vmem("back0", (2 * tokens, rows))
+    vmem("back1", (2 * tokens, rows))
+    vmem("slot_gate", (rows, 1), F32)
+    vmem("gate_column", (2, 2 * tokens, 1), F32)
     vmem("x_in", (chunks, 2 * tokens, cw))
     vmem("gate", (rows, hidden), F32)
     vmem("up", (rows, hidden), F32)
@@ -652,18 +759,13 @@
     vmem("da_tan", (rows // 2, hidden), F32)
     vmem("db_tan", (rows // 2, hidden), F32)
     vmem("y_tan", (tokens, quarter), F32)
-    vmem("dx", (tokens, quarter))
-    run = N_MP * nz * per
-    vmem("prod", (N_CORE, ny, run, quarter))
-    vmem("core_in", (ny, run, quarter))
-    names.add("core_ssem", pltpu.SemaphoreType.DMA)
-    names.add("core_rsem", pltpu.SemaphoreType.DMA)
-    vmem("sum_y", (1, ny, run, quarter))
-    vmem("in_y", (1, ny, run, quarter))
-    sems("ex_y", 1, ny)
-    vmem("sum_z", (1, nz, N_MP * per, quarter))
-    vmem("in_z", (1, nz, N_MP * per, quarter))
-    sems("ex_z", 1, nz)
+    vmem("dx", (back_chunks, N_CORE, ny, tokens, 2 * bw))
+    sems("spread_y", back_chunks, ny)
+    names.add("core_ssem", pltpu.SemaphoreType.DMA((back_chunks,)))
+    names.add("core_rsem", pltpu.SemaphoreType.DMA((back_chunks,)))
+    vmem("sum_z", (back_chunks, nz, N_MP * per, 2 * bw))
+    vmem("in_z", (back_chunks, nz, N_MP * per, 2 * bw))
+    sems("ex_z", back_chunks, nz)
     vmem("last_a", (1, N_MP, per, quarter), F32)
     vmem("last_b", (1, N_MP, per, quarter), F32)
     sems("last", 1, N_MP)
@@ -675,34 +777,13 @@
     hidden = w_gate.shape[2]
     experts = nz * nyc
     cap = max(2, 5 * 2 * tokens // (4 * experts))
-    half = nyc * cap
-    rows = nz * 2 * half
     sizes = (nz, nyc, cap, tokens, quarter, hidden, CHUNKS, BACK_CHUNKS)
-
-    flat = routes.reshape(-1)
-    number = jnp.arange(flat.shape[0])
-    earlier = (flat[:, None] == flat[None, :]) & (number[None, :] < number[:, None])
-    slot = flat * cap + jnp.sum(earlier.astype(jnp.int32), axis=1)
-    place = (slot // half) * (2 * half) + slot % half
-    place = place.reshape(tokens, 2)
-    place = jnp.stack([place, place + half], 0).reshape(2 * tokens, 2)
-    line = jnp.arange(rows)
-    back0 = (place[:, 0:1] == line[None, :]).astype(BF)
-    back1 = (place[:, 1:2] == line[None, :]).astype(BF)
-    pick = ((line[:, None] == place[None, :, 0]) | (line[:, None] == place[None, :, 1])).astype(BF)
-    gates2 = jnp.concatenate([gates, gates], 0)
-    slot_gate = jnp.sum(
-        jnp.where(line[:, None] == place[None, :, 0], gates2[None, :, 0], 0.0)
-        + jnp.where(line[:, None] == place[None, :, 1], gates2[None, :, 1], 0.0),
-        axis=1,
-        keepdims=True,
-    )
     names = scratch(sizes)
     vmem, anywhere = pl.BlockSpec(memory_space=pltpu.VMEM), pl.BlockSpec(memory_space=pl.ANY)
     return pl.pallas_call(
         functools.partial(kernel, sizes, names),
         out_shape=jax.ShapeDtypeStruct((1, quarter // experts, N_MP * quarter), F32),
-        in_specs=[anywhere] * 3 + [vmem] * 7 + [anywhere] * 3,
+        in_specs=[anywhere] * 3 + [vmem] * 4 + [anywhere] * 3,
         out_specs=vmem,
         scratch_shapes=names.shapes,
         compiler_params=pltpu.CompilerParams(
@@ -710,7 +791,16 @@
         ),
         cost_estimate=pl.CostEstimate(flops=6_000_000_000, bytes_accessed=12_000_000, transcendentals=300_000),
     )(
-        attn, out_proj, tangent_proj, resid, target, pick, back0, back1, slot_gate, gates2, w_gate, w_up, w_down
+        attn,
+        out_proj,
+        tangent_proj,
+        resid,
+        target,
+        routes.T,
+        gates.T,
+        jnp.swapaxes(w_gate, 1, 2),
+        jnp.swapaxes(w_up, 1, 2),
+        w_down,
     )
 
 

time: 217 us -> 177 us (0.82)
  Pallas kernels: 205 us -> 176 us
  local copies, waits for them, and re-layouts: 8.91 us -> 1.47 us
  other arithmetic: 3.02 us -> 0 us
    pallas_call x1, Pallas kernels: 205 us -> 176 us  [local(): pl.pallas_call(functools.partial(kernel, sizes, names), out_shape=jax.Sha...]
    unnamed x9 -> x1, local copies, waits for them, and re-layouts: 6.2 us -> 1.47 us
where the time goes in v2:
time: 177 us
  Pallas kernels  176 us (99%)
    pallas_call x1, Pallas kernels, local(): pl.pallas_call(functools.partial(kernel, sizes, names), out_shape=jax.Sha...  176 us

profile of v2, /device:TPU:1, one launch (start us, length us, event | category | flops | bytes accessed | tf_op | source)
XLA Modules:
  0.0 177.2 jit_solution(12295997204733168260)
XLA Ops:
  0.0 175.7 %shard_map.100 = f32[1,8,2048]{2,1,0:T(8,128)} custom-call(bf16[128,512]{1,0:T(8,128)(2,1)} %refs_0_.1, bf16[512,2048]{1,0:T(8,128)(2,1)} %refs_1_.1, bf16[512,2048]{1,0:T(8,128)(2,1)} %refs_2_.1, bf16[128,512]{1,0:T(8,128)(2,1)} %refs_3_.1, bf16[128,512]{1,0:T(8,128)(2,1)} %refs_4_.1, s32[2,128]{1,0:T(2,128)} %bitcast.6, f32[2,128]{1,0:T(2,128)} %bitcast.7, ...), custom_call_target="tpu_custom_call" | custom-call | flops 6000000000 | bytes 12000000 | tf_op jit(solution)/shard_map/pallas_call | solution.py:783
  175.7 1.5 copy.12

commit v3 on v2

--- a/solution.py
+++ b/solution.py
@@ -15,9 +15,29 @@
 N_CORE = 2
 CHUNKS = 4
 BACK_CHUNKS = 2
-ORDER_IN = (2, 3, 2, 1, 0, 2, 0, 1, 1, 2, 3, 1, 0, 3, 2, 3, 0, 1, 2, 1, 3, 2, 0, 1, 3, 0, 3, 1, 2, 0, 3, 0)
-ORDER_OUT = (0, 3, 0, 0, 3, 3, 0, 2, 2, 3, 1, 0, 2, 3, 1, 1, 2, 0, 3, 1, 2, 1, 0, 3, 2, 3, 0, 1, 2, 3, 0, 1, 2, 1, 2, 1, 3, 0, 2, 1)
-ORDER_BACK = (0, 0, 1, 0, 1, 1, 0, 1, 0, 1, 0, 1, 0, 0, 1, 1, 0, 1)
+PARTS = 2
+ORDER = (
+    ("z1", 3, 0), ("z1", 1, 0), ("z2", 3, 0), ("z1", 2, 0), ("zm", 3, 0), ("z2", 1, 0), ("z1", 0, 0),
+    ("zm", 1, 0), ("sp", 3, 0), ("z2", 2, 0), ("zm", 2, 0), ("z2", 0, 0), ("sp", 1, 0), ("zm", 0, 0),
+    ("sp", 0, 0), ("pa", 3, 0), ("sp", 2, 0), ("pa", 1, 0), ("gs", 3, 0), ("gs", 3, 1), ("pa", 0, 0),
+    ("gs", 1, 0), ("gm", 3, 0), ("gs", 1, 1), ("pa", 2, 0), ("gs", 0, 0), ("gm", 1, 0), ("pr", 3, 0),
+    ("gs", 2, 0), ("gm", 0, 0), ("gs", 2, 1), ("gm", 2, 0), ("gs", 0, 1), ("gm", 3, 1), ("pr", 0, 0),
+    ("pr", 1, 0), ("gm", 1, 1), ("gm", 2, 1), ("pr", 2, 0), ("ac", 0, 0), ("gm", 0, 1), ("o1", 2, 0),
+    ("o1", 1, 0), ("o1", 3, 0), ("o2", 1, 0), ("pr", 3, 1), ("pr", 1, 1), ("pr", 2, 1), ("pr", 0, 1),
+    ("ac", 0, 1), ("o1", 1, 1), ("om", 1, 0), ("o1", 2, 1), ("o2", 1, 1), ("om", 1, 1), ("o2", 2, 1),
+    ("o2", 2, 0), ("om", 2, 0), ("o2", 3, 0), ("om", 2, 1), ("om", 3, 0), ("o1", 0, 0), ("o1", 3, 1),
+    ("rt", 1, 0), ("o1", 0, 1), ("rt", 2, 0), ("po", 1, 0), ("o2", 0, 1), ("o2", 3, 1), ("om", 3, 1),
+    ("po", 2, 0), ("o2", 0, 0), ("om", 0, 0), ("rt", 3, 0), ("re", 1, 0), ("om", 0, 1), ("po", 3, 0),
+    ("re", 2, 0), ("rt", 0, 0), ("pc", 1, 0), ("po", 0, 0), ("re", 3, 0), ("cs", 1, 0), ("cs", 1, 1),
+    ("pc", 2, 0), ("re", 0, 0), ("cm", 1, 0), ("cs", 2, 0), ("cs", 2, 1), ("cm", 1, 1), ("pc", 3, 0),
+    ("cm", 2, 0), ("cm", 2, 1), ("pc", 0, 0), ("cs", 3, 0), ("cs", 3, 1), ("cm", 3, 0), ("cs", 0, 0),
+    ("dh", 2, 0), ("cs", 0, 1), ("dh", 1, 1), ("cm", 0, 0), ("dh", 3, 0), ("cm", 3, 1), ("dh", 1, 0),
+    ("dh", 2, 1), ("cm", 0, 1), ("dh", 0, 0), ("ta", 0, 0), ("b1", 0, 0), ("b1", 1, 0), ("dh", 0, 1),
+    ("dh", 3, 1), ("ta", 0, 1), ("b1", 0, 1), ("b1", 1, 1), ("b2", 0, 0), ("bm", 0, 0), ("b2", 0, 1),
+    ("bm", 0, 1), ("b2", 1, 1), ("b2", 1, 0), ("bm", 1, 1), ("bm", 1, 0), ("br", 0, 0), ("br", 1, 0),
+    ("pb", 0, 0), ("pb", 1, 0), ("dx", 0, 0), ("dx", 1, 0), ("dc", 0, 0), ("pd", 0, 0), ("dc", 1, 0),
+    ("pd", 1, 0), ("tz", 0, 0), ("tz", 1, 0),
+)
 
 
 class Names:
@@ -59,13 +79,6 @@
         return carry
 
     lax.fori_loop(lower, upper, step, 0)
-
-
-def pipeline(stages, order):
-    done = [0] * (max(order) + 1)
-    for k in order:
-        stages[done[k]](k)
-        done[k] += 1
 
 
 class Exchange:
@@ -146,15 +159,19 @@
 
 
 class Scatter:
-    def __init__(self, ring, part, hop, total, sems, rows):
-        self.ring, self.part, self.hop, self.total, self.rows = ring, part, hop, total, rows
+    def __init__(self, ring, part, hop, total, sems, rows, parts):
+        self.ring, self.part, self.hop, self.total = ring, part, hop, total
+        self.rows, self.parts = rows // parts, parts
+        self.half = self.rows // 2
         self.ssem, self.rsem = sems
-        self.half = rows // 2
-
-    def copy(self, k, i):
-        r, h = self.ring, self.half
-        first, second = pl.ds(0, h), pl.ds(h, h)
-        part, hop, total = self.part.at[k], self.hop.at[k], self.total.at[k]
+
+    def halves(self, b):
+        return pl.ds(b * self.rows, self.half), pl.ds(b * self.rows + self.half, self.half)
+
+    def copy(self, k, b, i):
+        r, j = self.ring, k * self.parts + b
+        first, second = self.halves(b)
+        part, hop, total = self.part.at[k], self.hop.at[j], self.total.at[k]
         plan = (
             (part.at[r.opp, first], hop.at[0], r.left),
             (part.at[r.opp, second], hop.at[1], r.right),
@@ -164,87 +181,85 @@
             (part.at[r.right, second], total.at[1, second], r.right),
         )
         src, dst, to = plan[i]
-        return r.copy(src, dst, self.ssem.at[k, i], self.rsem.at[k, i], to)
-
-    def start(self, k, index):
-        self.copy(k, index).start()
-
-    def middle(self, k):
-        r, h = self.ring, self.half
-        self.copy(k, 0).wait_recv()
-        self.add(k, r.left, pl.ds(0, h), 0)
-        self.copy(k, 4).start()
-        self.copy(k, 1).wait_recv()
-        self.add(k, r.right, pl.ds(h, h), 1)
-        self.copy(k, 5).start()
-
-    def add(self, k, block, rows, side):
-        value = self.part[k, pl.ds(block, 1), rows, :][0].astype(F32) + self.hop[k, side].astype(F32)
+        return r.copy(src, dst, self.ssem.at[j, i], self.rsem.at[j, i], to)
+
+    def start(self, k, b, index):
+        self.copy(k, b, index).start()
+
+    def middle(self, k, b=0):
+        r = self.ring
+        first, second = self.halves(b)
+        self.copy(k, b, 0).wait_recv()
+        self.add(k, b, r.left, first, 0)
+        self.copy(k, b, 4).start()
+        self.copy(k, b, 1).wait_recv()
+        self.add(k, b, r.right, second, 1)
+        self.copy(k, b, 5).start()
+
+    def add(self, k, b, block, rows, side):
+        hop = self.hop[k * self.parts + b, side].astype(F32)
+        value = self.part[k, pl.ds(block, 1), rows, :][0].astype(F32) + hop
         self.part[k, pl.ds(block, 1), rows, :] = value.astype(BF)[None]
 
-    def finish(self, k):
+    def finish(self, k, b=0):
         for i in (2, 3, 4, 5):
-            self.copy(k, i).wait_recv()
-        own = self.part[k, pl.ds(self.ring.me, 1)][0].astype(F32)
-        return own + self.total[k, 0].astype(F32) + self.total[k, 1].astype(F32)
+            self.copy(k, b, i).wait_recv()
+        rows = pl.ds(b * self.rows, self.rows)
+        own = self.part[k, pl.ds(self.ring.me, 1), rows, :][0].astype(F32)
+        return own + self.total[k, 0, rows, :].astype(F32) + self.total[k, 1, rows, :].astype(F32)
 
     def drain(self, k):
-        for i in range(6):
-            self.copy(k, i).wait_send()
+        for b in range(self.parts):
+            for i in range(6):
+                self.copy(k, b, i).wait_send()
 
 
 class Gather:
-    def __init__(self, ring, full, sems, rows):
+    def __init__(self, ring, full, sems, rows, parts):
         self.ring, self.full = ring, full
+        self.rows, self.parts = rows // parts, parts
+        self.half = self.rows // 2
         self.ssem, self.rsem = sems
-        self.half = rows // 2
-
-    def move(self, k, i, block, rows, to):
-        ref = self.full.at[k, block, rows]
-        return self.ring.copy(ref, ref, self.ssem.at[k, i], self.rsem.at[k, i], to)
-
-    def copy(self, k, i):
-        r, h = self.ring, self.half
-        first, second = pl.ds(0, h), pl.ds(h, h)
+
+    def move(self, k, b, i, block, side, to):
+        ref = self.full.at[k, block, pl.ds(b * self.rows + side * self.half, self.half)]
+        j = k * self.parts + b
+        return self.ring.copy(ref, ref, self.ssem.at[j, i], self.rsem.at[j, i], to)
+
+    def copy(self, k, b, i):
+        r = self.ring
         plan = (
-            (r.me, first, r.left),
-            (r.me, second, r.right),
-            (r.me, second, r.left),
-            (r.me, first, r.right),
-            (r.right, first, r.left),
-            (r.left, second, r.right),
+            (r.me, 0, r.left),
+            (r.me, 1, r.right),
+            (r.me, 1, r.left),
+            (r.me, 0, r.right),
+            (r.right, 0, r.left),
+            (r.left, 1, r.right),
         )
-        return self.move(k, i, *plan[i])
-
-    def arrival(self, k, i):
-        r, h = self.ring, self.half
-        first, second = pl.ds(0, h), pl.ds(h, h)
-        plan = (
-            (r.right, first),
-            (r.left, second),
-            (r.right, second),
-            (r.left, first),
-            (r.opp, first),
-            (r.opp, second),
-        )
-        return self.move(k, i, *plan[i], r.left)
-
-    def start(self, k):
+        return self.move(k, b, i, *plan[i])
+
+    def arrival(self, k, b, i):
+        r = self.ring
+        plan = ((r.right, 0), (r.left, 1), (r.right, 1), (r.left, 0), (r.opp, 0), (r.opp, 1))
+        return self.move(k, b, i, *plan[i], r.left)
+
+    def start(self, k, b=0):
         for i in range(4):
-            self.copy(k, i).start()
-
-    def middle(self, k):
+            self.copy(k, b, i).start()
+
+    def middle(self, k, b=0):
         for i in range(2):
-            self.arrival(k, i).wait_recv()
-            self.copy(k, 4 + i).start()
-
-    def finish(self, k):
+            self.arrival(k, b, i).wait_recv()
+            self.copy(k, b, 4 + i).start()
+
+    def finish(self, k, b=0):
         for i in range(2, 6):
-            self.arrival(k, i).wait_recv()
+            self.arrival(k, b, i).wait_recv()
 
     def drain(self, k):
-        for i in range(6):
-            self.copy(k, i).wait_send()
+        for b in range(self.parts):
+            for i in range(6):
+                self.copy(k, b, i).wait_send()
 
 
 def iota(shape, dim):
@@ -308,21 +323,21 @@
     def sems(name):
         return getattr(s, name + "_ssem"), getattr(s, name + "_rsem")
 
-    scat_z = Scatter(ring, s.part_z, s.hop_z, s.total_z, sems("scat_z"), 2 * tokens)
+    scat_z = Scatter(ring, s.part_z, s.hop_z, s.total_z, sems("scat_z"), 2 * tokens, 1)
     go_z = Exchange(s.go_a, s.go_b, sems("go_z"), nz, z, at_z)
     go_yc = Exchange(s.go_c, s.go_d, sems("go_yc"), nyc, yc, at_yc)
-    gather_x = Gather(ring, s.x_full, sems("gather_x"), rows)
-    scat_o = Scatter(ring, s.part_o, s.hop_o, s.total_o, sems("scat_o"), rows)
+    gather_x = Gather(ring, s.x_full, sems("gather_x"), rows, PARTS)
+    scat_o = Scatter(ring, s.part_o, s.hop_o, s.total_o, sems("scat_o"), rows, PARTS)
     ret_yc = Exchange(s.ret_a, s.ret_b, sems("ret_yc"), nyc, yc, at_yc)
     ret_z = Exchange(s.ret_c, s.ret_d, sems("ret_z"), nz, z, at_z)
     cot_z = Exchange(s.cot_a, s.cot_b, sems("cot_z"), nz, z, at_z)
     cot_yc = Exchange(s.cot_c, s.cot_d, sems("cot_yc"), nyc, yc, at_yc)
-    gather_c = Gather(ring, s.c_full, sems("gather_c"), rows)
-    scat_b = Scatter(ring, s.part_b, s.hop_b, s.total_b, sems("scat_b"), rows)
+    gather_c = Gather(ring, s.c_full, sems("gather_c"), rows, PARTS)
+    scat_b = Scatter(ring, s.part_b, s.hop_b, s.total_b, sems("scat_b"), rows, PARTS)
     bak_yc = Exchange(s.bak_a, s.bak_b, sems("bak_yc"), nyc, yc, at_yc)
     bak_z = Exchange(s.bak_c, s.bak_d, sems("bak_z"), nz, z, at_z)
     att_yc = Exchange(s.att_a, s.att_b, sems("att_yc"), nyc, yc, at_yc)
-    gather_a = Gather(ring, s.att_full, sems("gather_a"), quarter)
+    gather_a = Gather(ring, s.att_full, sems("gather_a"), quarter, 1)
     spread_y = SpreadY(s.dx, core, sems("spread_y"), ny, y, lambda to: at_yc(to * N_CORE + core))
     ex_z = Exchange(s.sum_z, s.in_z, sems("ex_z"), nz, z, at_z)
     last = Exchange(s.last_a, s.last_b, sems("last"), N_MP, me_m, lambda to: (me_e, to))
@@ -331,30 +346,24 @@
         value = dot(s.swap[...], src[k].reshape(rows, width))
         dst[k] = value.astype(BF).reshape(nyc, block, width)
 
-    loads[0].wait()
-    loads[1].wait()
-    loads[2].wait()
+    per = quarter // (nz * nyc)
+    run = nz * per
+    part_rows, part_blocks = rows // PARTS, nyc // PARTS
 
     def z_part(k, q):
         columns = pl.ds(pl.multiple_of(q * quarter + k * cw, 128), cw)
         s.part_z[k, pl.ds(q, 1), pl.ds(0, tokens), :] = dot(s.attn[...], s.out_proj[:, columns]).astype(BF)[None]
         s.part_z[k, pl.ds(q, 1), pl.ds(tokens, tokens), :] = dot(s.attn[...], s.tan_proj[:, columns]).astype(BF)[None]
 
-    def z_first(k):
-        z_part(k, ring.opp)
-        if nth("z_first") == 0:
-            pl.semaphore_wait(barrier, nz + nyc + N_MP - 3)
-        scat_z.start(k, 0)
-        scat_z.start(k, 1)
-
-    def z_second(k):
-        z_part(k, ring.left)
-        scat_z.start(k, 2)
-        z_part(k, ring.right)
-        scat_z.start(k, 3)
-        z_part(k, ring.me)
-        if nth("z_second") == 0:
-            route_rows()
+    def z_first(k, _):
+        scat_z.start(k, 0, 0)
+        scat_z.start(k, 0, 1)
+
+    def z_second(k, _):
+        scat_z.start(k, 0, 2)
+        scat_z.start(k, 0, 3)
+        if nth("z_second") == chunks - 1:
+            att_yc.start(0)
 
     def route_rows():
         eye = iota((tokens, tokens), 0) == iota((tokens, tokens), 1)
@@ -417,7 +426,7 @@
         a, h, b, p = r // block, (r % block) // half, (r % half) // cap, r % cap
         s.swap[...] = (iota((rows, rows), 1) == b * block + h * half + a * cap + p).astype(F32).astype(BF)
 
-    def spread_x(k):
+    def spread_x(k, _):
         value = scat_z.finish(k)
         columns = pl.ds(k * cw, cw)
         s.x_in[k, pl.ds(0, tokens), :] = (
@@ -426,33 +435,35 @@
         s.x_in[k, pl.ds(tokens, tokens), :] = value[tokens:].astype(BF)
         s.go_a[k] = dot(s.pick[...], s.x_in[k]).astype(BF).reshape(nz, block, cw)
         go_z.start(k)
-        before = nth("spread_x")
-        if before == 0:
-            swap_rows()
-        if before == chunks - 1:
-            attn_send()
-
-    def pass_x(k):
+        if nth("spread_x") == chunks - 1:
+            att_yc.wait(0)
+            s.att_full[0, pl.ds(me_m, 1)] = s.att_b[0].reshape(1, nyc * run, tokens)
+            gather_a.start(0)
+
+    def pass_x(k, _):
         go_z.wait(k)
         swap(s.go_b, s.go_c, k, cw)
         go_yc.start(k)
-
-    def gather_start_x(k):
-        go_yc.wait(k)
-        s.x_full[k, pl.ds(me_m, 1)] = s.go_d[k].reshape(1, rows, cw)
-        gather_x.start(k)
+        if nth("pass_x") == chunks - 1:
+            gather_a.middle(0)
+
+    def gather_start_x(k, b):
+        if b == 0:
+            go_yc.wait(k)
+            s.x_full[k, pl.ds(me_m, 1)] = s.go_d[k].reshape(1, rows, cw)
+        gather_x.start(k, b)
 
     step_rows = 2 * block
 
-    def pre_acts(k):
-        gather_x.finish(k)
-        before = nth("pre_acts")
-        if before == 0:
+    def pre_acts(k, b):
+        gather_x.finish(k, b)
+        before = nth(("pre_acts", b))
+        if nth("pre_acts") == 0:
             loads[3].wait()
             loads[4].wait()
 
         def body(i):
-            at = pl.ds(pl.multiple_of(i * step_rows, step_rows), step_rows)
+            at = pl.ds(pl.multiple_of(b * part_rows + i * step_rows, step_rows), step_rows)
             gate = jnp.zeros((step_rows, hidden), F32)
             up = jnp.zeros((step_rows, hidden), F32)
             for m in range(N_MP):
@@ -466,26 +477,14 @@
             s.gate[at, :] = gate
             s.up[at, :] = up
 
-        each(0, rows // step_rows, body)
-
-    per = quarter // (nz * nyc)
-    run = nz * per
-
-    def attn_send():
+        each(0, part_rows // step_rows, body)
+
+    def attn_blocks():
         r = iota((quarter, 1), 0)
         c, zz, p = r // run, (r % run) // per, r % per
         wanted = (zz * nyc + c) * per + p
         permute = (iota((quarter, quarter), 1) == wanted).astype(F32).astype(BF)
         s.att_a[0] = dot_last(permute, s.attn[...]).astype(BF).reshape(nyc, run, tokens)
-        att_yc.start(0)
-
-    def attn_gather():
-        att_yc.wait(0)
-        s.att_full[0, pl.ds(me_m, 1)] = s.att_b[0].reshape(1, nyc * run, tokens)
-        gather_a.start(0)
-
-    pipeline((z_first, z_second, scat_z.middle, spread_x, pass_x, gather_start_x, gather_x.middle, pre_acts), ORDER_IN)
-    attn_gather()
 
     def activations(i):
         at, tan_at = pl.ds(pl.multiple_of(i * block, 8), half), pl.ds(pl.multiple_of(i * block + half, 8), half)
@@ -496,30 +495,35 @@
         hid_tan = silu_one * gate_tan * up_pre + silu_val * up_tan
         s.hidden[pl.ds(pl.multiple_of(i * block, 16), block), :] = jnp.concatenate([hid, hid_tan], 0).astype(BF)
 
-    each(0, nyc, activations)
-    loads[5].wait()
-
-    def o_part(k, q):
+    def hidden_units(_, b):
+        each(b * part_blocks, (b + 1) * part_blocks, activations)
+        if nth("hidden_units") == 0:
+            loads[5].wait()
+
+    def o_part(k, b, q):
         columns = pl.ds(pl.multiple_of(q * quarter + k * cw, 128), cw)
-        s.part_o[k, pl.ds(q, 1)] = dot(s.hidden[...], s.w_down[:, columns]).astype(BF)[None]
-
-    def o_first(k):
-        o_part(k, ring.opp)
-        scat_o.start(k, 0)
-        scat_o.start(k, 1)
-
-    def o_second(k):
-        o_part(k, ring.left)
-        scat_o.start(k, 2)
-        o_part(k, ring.right)
-        scat_o.start(k, 3)
-        o_part(k, ring.me)
-
-    def return_o(k):
-        s.ret_a[k] = scat_o.finish(k).astype(BF).reshape(nyc, block, cw)
+        at = pl.ds(b * part_rows, part_rows)
+        s.part_o[k, pl.ds(q, 1), at, :] = dot(s.hidden[at, :], s.w_down[:, columns]).astype(BF)[None]
+
+    def o_first(k, b):
+        o_part(k, b, ring.opp)
+        scat_o.start(k, b, 0)
+        scat_o.start(k, b, 1)
+
+    def o_second(k, b):
+        o_part(k, b, ring.left)
+        scat_o.start(k, b, 2)
+        o_part(k, b, ring.right)
+        scat_o.start(k, b, 3)
+        o_part(k, b, ring.me)
+
+    def return_o(k, _):
+        for b in range(PARTS):
+            value = scat_o.finish(k, b).astype(BF)
+            s.ret_a[k, pl.ds(b * part_blocks, part_blocks)] = value.reshape(part_blocks, block, cw)
         ret_yc.start(k)
 
-    def pass_o(k):
+    def pass_o(k, _):
         ret_yc.wait(k)
         swap(s.ret_b, s.ret_c, k, cw)
         ret_z.start(k)
@@ -527,7 +531,7 @@
     def combine(values):
         return s.gate_column[0] * dot(s.back0[...], values) + s.gate_column[1] * dot(s.back1[...], values)
 
-    def residual(k):
+    def residual(k, _):
         ret_z.wait(k)
         columns = pl.ds(k * cw, cw)
         both = s.x_in[k].astype(F32) + combine(s.ret_d[k].reshape(rows, cw))
@@ -537,22 +541,23 @@
         s.cot_a[k] = (dot(s.pick[...], sent) * s.slot_gate[...]).astype(BF).reshape(nz, block, cw)
         cot_z.start(k)
 
-    def pass_c(k):
+    def pass_c(k, _):
         cot_z.wait(k)
         swap(s.cot_b, s.cot_c, k, cw)
         cot_yc.start(k)
 
-    def gather_start_c(k):
-        cot_yc.wait(k)
-        s.c_full[k, pl.ds(me_m, 1)] = s.cot_d[k].reshape(1, rows, cw)
-        gather_c.start(k)
-
-    def grad_hidden(k):
-        gather_c.finish(k)
-        before = nth("grad_hidden")
+    def gather_start_c(k, b):
+        if b == 0:
+            cot_yc.wait(k)
+            s.c_full[k, pl.ds(me_m, 1)] = s.cot_d[k].reshape(1, rows, cw)
+        gather_c.start(k, b)
+
+    def grad_hidden(k, b):
+        gather_c.finish(k, b)
+        before = nth(("grad_hidden", b))
 
         def body(i):
-            at = pl.ds(pl.multiple_of(i * step_rows, step_rows), step_rows)
+            at = pl.ds(pl.multiple_of(b * part_rows + i * step_rows, step_rows), step_rows)
             grad = jnp.zeros((step_rows, hidden), F32)
             for m in range(N_MP):
                 features = pl.ds(m * quarter + k * cw, cw)
@@ -561,24 +566,7 @@
                 grad = grad + s.grad[at, :]
             s.grad[at, :] = grad
 
-        each(0, rows // step_rows, body)
-
-    pipeline(
-        (
-            o_first,
-            o_second,
-            scat_o.middle,
-            return_o,
-            pass_o,
-            residual,
-            pass_c,
-            gather_start_c,
-            gather_c.middle,
-            grad_hidden,
-        ),
-        ORDER_OUT,
-    )
-    gather_a.middle(0)
+        each(0, part_rows // step_rows, body)
 
     def tangents(i):
         at, tan_at = pl.ds(pl.multiple_of(i * block, 8), half), pl.ds(pl.multiple_of(i * block + half, 8), half)
@@ -592,39 +580,44 @@
         s.da_tan[to, :] = da_tan
         s.db_tan[to, :] = db_tan
 
-    each(0, nyc, tangents)
-
-    def b_part(k, q):
-        da_tan, db_tan = s.da_tan[...].astype(BF), s.db_tan[...].astype(BF)
+    def tangent_units(_, b):
+        each(b * part_blocks, (b + 1) * part_blocks, tangents)
+
+    def b_part(k, b, q):
+        at = pl.ds(b * part_rows // 2, part_rows // 2)
+        da_tan, db_tan = s.da_tan[at, :].astype(BF), s.db_tan[at, :].astype(BF)
         sides = []
         for h in range(2):
             features = pl.ds(pl.multiple_of(q * quarter + h * (quarter // 2) + k * bw, 128), bw)
             term = dot(da_tan, s.w_gate[:, features]) + dot(db_tan, s.w_up[:, features])
-            sides.append(term.reshape(nyc, half, bw))
-        s.part_b[k, pl.ds(q, 1)] = jnp.concatenate(sides, 1).astype(BF).reshape(1, rows, bw)
-
-    def b_first(k):
-        b_part(k, ring.opp)
-        scat_b.start(k, 0)
-        scat_b.start(k, 1)
-
-    def b_second(k):
-        b_part(k, ring.left)
-        scat_b.start(k, 2)
-        b_part(k, ring.right)
-        scat_b.start(k, 3)
-        b_part(k, ring.me)
-
-    def return_b(k):
-        s.bak_a[k] = scat_b.finish(k).astype(BF).reshape(nyc, block, bw)
+            sides.append(term.reshape(part_blocks, half, bw))
+        value = jnp.concatenate(sides, 1).astype(BF).reshape(1, part_rows, bw)
+        s.part_b[k, pl.ds(q, 1), pl.ds(b * part_rows, part_rows), :] = value
+
+    def b_first(k, b):
+        b_part(k, b, ring.opp)
+        scat_b.start(k, b, 0)
+        scat_b.start(k, b, 1)
+
+    def b_second(k, b):
+        b_part(k, b, ring.left)
+        scat_b.start(k, b, 2)
+        b_part(k, b, ring.right)
+        scat_b.start(k, b, 3)
+        b_part(k, b, ring.me)
+
+    def return_b(k, _):
+        for b in range(PARTS):
+            value = scat_b.finish(k, b).astype(BF)
+            s.bak_a[k, pl.ds(b * part_blocks, part_blocks)] = value.reshape(part_blocks, block, bw)
         bak_yc.start(k)
 
-    def pass_b(k):
+    def pass_b(k, _):
         bak_yc.wait(k)
         swap(s.bak_b, s.bak_c, k, bw)
         bak_z.start(k)
 
-    def grad_in(k):
+    def grad_in(k, _):
         bak_z.wait(k)
         both = combine(s.bak_d[k].reshape(rows, bw))
         for h in range(2):
@@ -645,7 +638,7 @@
             device_id_type=MESH,
         )
 
-    def dx_core(k):
+    def dx_core(k, _):
         spread_y.wait(k)
         core_copy(k, core).start()
 
@@ -658,7 +651,7 @@
                     source = pl.ds((yy * N_CORE + c) * run, run)
                     s.att_rows[pl.ds(m * run, run), columns] = s.att_full[0, m, source, :]
 
-    def product(k):
+    def product(k, _):
         if nth("product") == 0:
             attn_rows()
         core_copy(k, other).wait_recv()
@@ -668,7 +661,7 @@
         s.sum_z[k] = value.reshape(nz, N_MP * per, 2 * bw).astype(BF)
         ex_z.start(k)
 
-    def total_z(k):
+    def total_z(k, _):
         ex_z.wait(k)
         total = jnp.sum(s.in_z[k].astype(F32), axis=0) * (1.0 / math.sqrt(tokens * nz * nyc))
         total = total.reshape(N_MP, per, 2 * bw)
@@ -676,10 +669,49 @@
             columns = pl.ds(h * (quarter // 2) + k * bw, bw)
             s.last_a[0, :, :, columns] = total[:, :, h * bw : (h + 1) * bw]
 
-    pipeline(
-        (b_first, b_second, scat_b.middle, return_b, pass_b, grad_in, dx_core, product, total_z),
-        ORDER_BACK,
-    )
+    route_rows()
+    swap_rows()
+    loads[0].wait()
+    attn_blocks()
+    loads[1].wait()
+    loads[2].wait()
+    for k in range(chunks):
+        for q in (ring.opp, ring.left, ring.right, ring.me):
+            z_part(k, q)
+    pl.semaphore_wait(barrier, nz + nyc + N_MP - 3)
+    stages = {
+        "z1": z_first,
+        "z2": z_second,
+        "zm": scat_z.middle,
+        "sp": spread_x,
+        "pa": pass_x,
+        "gs": gather_start_x,
+        "gm": gather_x.middle,
+        "pr": pre_acts,
+        "ac": hidden_units,
+        "o1": o_first,
+        "o2": o_second,
+        "om": scat_o.middle,
+        "rt": return_o,
+        "po": pass_o,
+        "re": residual,
+        "pc": pass_c,
+        "cs": gather_start_c,
+        "cm": gather_c.middle,
+        "dh": grad_hidden,
+        "ta": tangent_units,
+        "b1": b_first,
+        "b2": b_second,
+        "bm": scat_b.middle,
+        "br": return_b,
+        "pb": pass_b,
+        "dx": grad_in,
+        "dc": dx_core,
+        "pd": product,
+        "tz": total_z,
+    }
+    for stage, k, b in ORDER:
+        stages[stage](k, b)
     last.start(0)
     last.wait(0)
     for m in range(N_MP):
@@ -728,9 +760,10 @@
         ("b", back_chunks, rows, bw),
     ):
         vmem("part_" + tag, (count, N_MP, height, width))
-        vmem("hop_" + tag, (count, 2, height // 2, width))
+        parts = 1 if tag == "z" else PARTS
+        vmem("hop_" + tag, (count * parts, 2, height // 2 // parts, width))
         vmem("total_" + tag, (count, 2, height, width))
-        sems("scat_" + tag, count, 6)
+        sems("scat_" + tag, count * parts, 6)
     for tag, count, width in (("go", chunks, cw), ("ret", chunks, cw), ("cot", chunks, cw), ("bak", back_chunks, bw)):
         for letter in "abcd":
             vmem(f"{tag}_{letter}", (count, nz, block, width))
@@ -738,7 +771,7 @@
         sems(tag + "_yc", count, nyc)
     for tag in "xc":
         vmem(tag + "_full", (chunks, N_MP, rows, cw))
-        sems("gather_" + tag, chunks, 6)
+        sems("gather_" + tag, chunks * PARTS, 6)
     run = nz * per
     for letter in "ab":
         vmem("att_" + letter, (1, nyc, run, tokens))

time: 177 us -> 175 us (0.989)
  Pallas kernels: 176 us -> 173 us
    pallas_call x1, Pallas kernels: 176 us -> 173 us  [local(): pl.pallas_call(functools.partial(kernel, sizes, names), out_shape=jax.Sha...]
where the time goes in v3:
time: 175 us
  Pallas kernels  173 us (99%)
    pallas_call x1, Pallas kernels, local(): pl.pallas_call(functools.partial(kernel, sizes, names), out_shape=jax.Sha...  173 us

profile of v3, /device:TPU:1, one launch (start us, length us, event | category | flops | bytes accessed | tf_op | source)
XLA Modules:
  0.0 174.7 jit_solution(15538092843874369221)
XLA Ops:
  0.0 173.2 %shard_map.100 = f32[1,8,2048]{2,1,0:T(8,128)} custom-call(bf16[128,512]{1,0:T(8,128)(2,1)} %refs_0_.1, bf16[512,2048]{1,0:T(8,128)(2,1)} %refs_1_.1, bf16[512,2048]{1,0:T(8,128)(2,1)} %refs_2_.1, bf16[128,512]{1,0:T(8,128)(2,1)} %refs_3_.1, bf16[128,512]{1,0:T(8,128)(2,1)} %refs_4_.1, s32[2,128]{1,0:T(2,128)} %bitcast.6, f32[2,128]{1,0:T(2,128)} %bitcast.7, ...), custom_call_target="tpu_custom_call" | custom-call | flops 6000000000 | bytes 12000000 | tf_op jit(solution)/shard_map/pallas_call | solution.py:816
  173.2 1.5 copy.12

commit v4 on v3

--- a/solution.py
+++ b/solution.py
@@ -17,24 +17,24 @@
 BACK_CHUNKS = 2
 PARTS = 2
 ORDER = (
-    ("z1", 3, 0), ("z1", 1, 0), ("z2", 3, 0), ("z1", 2, 0), ("zm", 3, 0), ("z2", 1, 0), ("z1", 0, 0),
-    ("zm", 1, 0), ("sp", 3, 0), ("z2", 2, 0), ("zm", 2, 0), ("z2", 0, 0), ("sp", 1, 0), ("zm", 0, 0),
-    ("sp", 0, 0), ("pa", 3, 0), ("sp", 2, 0), ("pa", 1, 0), ("gs", 3, 0), ("gs", 3, 1), ("pa", 0, 0),
-    ("gs", 1, 0), ("gm", 3, 0), ("gs", 1, 1), ("pa", 2, 0), ("gs", 0, 0), ("gm", 1, 0), ("pr", 3, 0),
-    ("gs", 2, 0), ("gm", 0, 0), ("gs", 2, 1), ("gm", 2, 0), ("gs", 0, 1), ("gm", 3, 1), ("pr", 0, 0),
-    ("pr", 1, 0), ("gm", 1, 1), ("gm", 2, 1), ("pr", 2, 0), ("ac", 0, 0), ("gm", 0, 1), ("o1", 2, 0),
-    ("o1", 1, 0), ("o1", 3, 0), ("o2", 1, 0), ("pr", 3, 1), ("pr", 1, 1), ("pr", 2, 1), ("pr", 0, 1),
-    ("ac", 0, 1), ("o1", 1, 1), ("om", 1, 0), ("o1", 2, 1), ("o2", 1, 1), ("om", 1, 1), ("o2", 2, 1),
-    ("o2", 2, 0), ("om", 2, 0), ("o2", 3, 0), ("om", 2, 1), ("om", 3, 0), ("o1", 0, 0), ("o1", 3, 1),
-    ("rt", 1, 0), ("o1", 0, 1), ("rt", 2, 0), ("po", 1, 0), ("o2", 0, 1), ("o2", 3, 1), ("om", 3, 1),
-    ("po", 2, 0), ("o2", 0, 0), ("om", 0, 0), ("rt", 3, 0), ("re", 1, 0), ("om", 0, 1), ("po", 3, 0),
-    ("re", 2, 0), ("rt", 0, 0), ("pc", 1, 0), ("po", 0, 0), ("re", 3, 0), ("cs", 1, 0), ("cs", 1, 1),
-    ("pc", 2, 0), ("re", 0, 0), ("cm", 1, 0), ("cs", 2, 0), ("cs", 2, 1), ("cm", 1, 1), ("pc", 3, 0),
-    ("cm", 2, 0), ("cm", 2, 1), ("pc", 0, 0), ("cs", 3, 0), ("cs", 3, 1), ("cm", 3, 0), ("cs", 0, 0),
-    ("dh", 2, 0), ("cs", 0, 1), ("dh", 1, 1), ("cm", 0, 0), ("dh", 3, 0), ("cm", 3, 1), ("dh", 1, 0),
-    ("dh", 2, 1), ("cm", 0, 1), ("dh", 0, 0), ("ta", 0, 0), ("b1", 0, 0), ("b1", 1, 0), ("dh", 0, 1),
-    ("dh", 3, 1), ("ta", 0, 1), ("b1", 0, 1), ("b1", 1, 1), ("b2", 0, 0), ("bm", 0, 0), ("b2", 0, 1),
-    ("bm", 0, 1), ("b2", 1, 1), ("b2", 1, 0), ("bm", 1, 1), ("bm", 1, 0), ("br", 0, 0), ("br", 1, 0),
+    ("z1", 3, 0), ("z1", 1, 0), ("z2", 3, 0), ("z1", 2, 0), ("zm", 3, 0), ("z2", 1, 0), ("zm", 1, 0),
+    ("z1", 0, 0), ("z2", 0, 0), ("sp", 3, 0), ("zm", 0, 0), ("sp", 1, 0), ("z2", 2, 0), ("sp", 0, 0),
+    ("zm", 2, 0), ("pa", 3, 0), ("sp", 2, 0), ("pa", 1, 0), ("gs", 3, 0), ("gs", 3, 1), ("pa", 0, 0),
+    ("gs", 1, 0), ("gs", 1, 1), ("gm", 3, 0), ("pa", 2, 0), ("gs", 0, 0), ("gm", 1, 0), ("gs", 2, 0),
+    ("gm", 0, 0), ("gs", 2, 1), ("gm", 2, 0), ("gs", 0, 1), ("gm", 1, 1), ("gm", 3, 1), ("pr", 3, 0),
+    ("gm", 2, 1), ("pr", 0, 0), ("pr", 1, 0), ("pr", 2, 0), ("ac", 0, 0), ("gm", 0, 1), ("o1", 1, 0),
+    ("o1", 2, 0), ("o2", 1, 0), ("pr", 1, 1), ("pr", 3, 1), ("pr", 2, 1), ("pr", 0, 1), ("ac", 0, 1),
+    ("o1", 1, 1), ("om", 1, 0), ("o1", 2, 1), ("o2", 1, 1), ("om", 1, 1), ("o2", 2, 0), ("o2", 2, 1),
+    ("om", 2, 1), ("o1", 3, 0), ("om", 2, 0), ("o1", 0, 0), ("o2", 3, 0), ("rt", 1, 0), ("o1", 3, 1),
+    ("om", 3, 0), ("rt", 2, 0), ("po", 1, 0), ("o2", 3, 1), ("o2", 0, 0), ("om", 3, 1), ("o1", 0, 1),
+    ("po", 2, 0), ("om", 0, 0), ("o2", 0, 1), ("rt", 3, 0), ("om", 0, 1), ("re", 1, 0), ("po", 3, 0),
+    ("re", 2, 0), ("rt", 0, 0), ("po", 0, 0), ("pc", 1, 0), ("re", 3, 0), ("pc", 2, 0), ("cs", 1, 0),
+    ("cs", 1, 1), ("re", 0, 0), ("cs", 2, 0), ("cs", 2, 1), ("cm", 1, 0), ("pc", 3, 0), ("cm", 2, 0),
+    ("cm", 1, 1), ("cm", 2, 1), ("pc", 0, 0), ("cs", 3, 0), ("cs", 3, 1), ("dh", 1, 1), ("dh", 2, 1),
+    ("cm", 3, 0), ("cs", 0, 0), ("cs", 0, 1), ("cm", 0, 0), ("cm", 3, 1), ("cm", 0, 1), ("dh", 2, 0),
+    ("dh", 1, 0), ("dh", 3, 0), ("dh", 0, 0), ("ta", 0, 0), ("b1", 0, 0), ("dh", 3, 1), ("b1", 1, 0),
+    ("dh", 0, 1), ("ta", 0, 1), ("b1", 0, 1), ("b2", 0, 0), ("bm", 0, 0), ("b1", 1, 1), ("b2", 0, 1),
+    ("bm", 0, 1), ("b2", 1, 1), ("b2", 1, 0), ("bm", 1, 0), ("bm", 1, 1), ("br", 0, 0), ("br", 1, 0),
     ("pb", 0, 0), ("pb", 1, 0), ("dx", 0, 0), ("dx", 1, 0), ("dc", 0, 0), ("pd", 0, 0), ("dc", 1, 0),
     ("pd", 1, 0), ("tz", 0, 0), ("tz", 1, 0),
 )
@@ -341,6 +341,11 @@
     spread_y = SpreadY(s.dx, core, sems("spread_y"), ny, y, lambda to: at_yc(to * N_CORE + core))
     ex_z = Exchange(s.sum_z, s.in_z, sems("ex_z"), nz, z, at_z)
     last = Exchange(s.last_a, s.last_b, sems("last"), N_MP, me_m, lambda to: (me_e, to))
+
+    def drain(count, *stages):
+        for k in range(count):
+            for stage in stages:
+                stage.drain(k)
 
     def swap(src, dst, k, width):
         value = dot(s.swap[...], src[k].reshape(rows, width))
@@ -527,6 +532,8 @@
         ret_yc.wait(k)
         swap(s.ret_b, s.ret_c, k, cw)
         ret_z.start(k)
+        if nth("pass_o") == chunks - 1:
+            drain(chunks, scat_z, go_z, go_yc, gather_x)
 
     def combine(values):
         return s.gate_column[0] * dot(s.back0[...], values) + s.gate_column[1] * dot(s.back1[...], values)
@@ -616,6 +623,9 @@
         bak_yc.wait(k)
         swap(s.bak_b, s.bak_c, k, bw)
         bak_z.start(k)
+        if nth("pass_b") == back_chunks - 1:
+            drain(chunks, scat_o, ret_yc, ret_z, cot_z, cot_yc, gather_c)
+            drain(1, att_yc, gather_a)
 
     def grad_in(k, _):
         bak_z.wait(k)
@@ -652,7 +662,8 @@
                     s.att_rows[pl.ds(m * run, run), columns] = s.att_full[0, m, source, :]
 
     def product(k, _):
-        if nth("product") == 0:
+        before = nth("product")
+        if before == 0:
             attn_rows()
         core_copy(k, other).wait_recv()
         value = dot(s.att_rows[...], s.dx[k].reshape(nyc * tokens, 2 * bw))
@@ -660,6 +671,8 @@
         value = jnp.stack([value[m] for m in range(N_MP)], 1)
         s.sum_z[k] = value.reshape(nz, N_MP * per, 2 * bw).astype(BF)
         ex_z.start(k)
+        if before == back_chunks - 1:
+            drain(back_chunks, scat_b, bak_yc, bak_z)
 
     def total_z(k, _):
         ex_z.wait(k)
@@ -717,15 +730,9 @@
     for m in range(N_MP):
         out[0, :, m * quarter : (m + 1) * quarter] = s.last_b[0, m]
 
-    for k in range(chunks):
-        for stage in (scat_z, go_z, go_yc, gather_x, scat_o, ret_yc, ret_z, cot_z, cot_yc, gather_c):
-            stage.drain(k)
+    drain(back_chunks, spread_y, ex_z)
     for k in range(back_chunks):
-        for stage in (scat_b, bak_yc, bak_z, spread_y, ex_z):
-            stage.drain(k)
         core_copy(k, core).wait_send()
-    att_yc.drain(0)
-    gather_a.drain(0)
     last.drain(0)
 
 

time: 175 us -> 172 us (0.983)
  Pallas kernels: 173 us -> 170 us
    pallas_call x1, Pallas kernels: 173 us -> 170 us  [local(): pl.pallas_call(functools.partial(kernel, sizes, names), out_shape=jax.Sha...]
where the time goes in v4:
time: 172 us
  Pallas kernels  170 us (99%)
    pallas_call x1, Pallas kernels, local(): pl.pallas_call(functools.partial(kernel, sizes, names), out_shape=jax.Sha...  170 us

profile of v4, /device:TPU:1, one launch (start us, length us, event | category | flops | bytes accessed | tf_op | source)
XLA Modules:
  0.0 171.7 jit_solution(9513064392007318903)
XLA Ops:
  0.0 170.2 %shard_map.100 = f32[1,8,2048]{2,1,0:T(8,128)} custom-call(bf16[128,512]{1,0:T(8,128)(2,1)} %refs_0_.1, bf16[512,2048]{1,0:T(8,128)(2,1)} %refs_1_.1, bf16[512,2048]{1,0:T(8,128)(2,1)} %refs_2_.1, bf16[128,512]{1,0:T(8,128)(2,1)} %refs_3_.1, bf16[128,512]{1,0:T(8,128)(2,1)} %refs_4_.1, s32[2,128]{1,0:T(2,128)} %bitcast.6, f32[2,128]{1,0:T(2,128)} %bitcast.7, ...), custom_call_target="tpu_custom_call" | custom-call | flops 6000000000 | bytes 12000000 | tf_op jit(solution)/shard_map/pallas_call | solution.py:823
  170.2 1.5 copy.12
